TPU v7x, 32 devices: a whole 2x2x4 slice. The times are simulated.
32 devices in a mesh: dp: 8 (over y, x, core), tensor: 4 (over z).
Axes of the slice: x: 2, y: 2, z: 4, core: 2. Of those that a mesh axis runs over, the one named last changes fastest.
Arguments:
- tokens: bfloat16 [1028, 8, 1024], P('tensor', 'dp'), may hold values from -6 to 6
- cotangent: bfloat16 [1028, 8, 1024], P('tensor', 'dp'), may hold values from -6 to 6
- image_valid: int32 [8], P('dp'), may hold values from 0 to 1, as said below
- key_mask: int32 [8, 1028], P('dp'), may hold values from 0 to 1, as said below
- patch_rows: int32 [8, 1028], P('dp'), may hold values from 0 to 31, as said below
- patch_cols: int32 [8, 1028], P('dp'), may hold values from 0 to 31, as said below
- first_gain: float32 [1024], replicated, may hold values from 0.25 to 1.75
- first_bias: float32 [1024], replicated, may hold values from -1.8 to 1.8
- input_weight: bfloat16 [3, 1024, 1024], P(None, 'dp', 'tensor'), may hold values from -0.1875 to 0.1875
- input_bias: float32 [2, 1024], P(None, 'tensor'), may hold values from -3 to 3
- output_weight: bfloat16 [1024, 1024], P('tensor', 'dp'), may hold values from -0.75 to 0.75
- output_bias: float32 [1024], replicated, may hold values from -1.8 to 1.8
- second_gain: float32 [1024], replicated, may hold values from 0.25 to 1.75
- second_bias: float32 [1024], replicated, may hold values from -1.8 to 1.8
- expand_weight: bfloat16 [2, 1024, 2736], P(None, 'dp', 'tensor'), may hold values from -0.1875 to 0.1875
- expand_bias: float32 [2, 2736], P(None, 'tensor'), may hold values from -3 to 3
- inner_gain: float32 [2736], P('tensor'), may hold values from 0.25 to 1.75
- inner_bias: float32 [2736], P('tensor'), may hold values from -1.8 to 1.8
- shrink_weight: bfloat16 [2736, 1024], P('tensor', 'dp'), may hold values from -0.109375 to 0.109375
- shrink_bias: float32 [1024], replicated, may hold values from -1.8 to 1.8
Outputs:
- result: bfloat16 [1028, 8, 1024], P('tensor', 'dp')
- tokens_gradient: float32 [1028, 8, 1024], P('tensor', 'dp')
- first_gain_gradient: float32 [1024], replicated
- first_bias_gradient: float32 [1024], replicated
- input_weight_gradient: float32 [3, 1024, 1024], P(None, 'dp', 'tensor')
- input_bias_gradient: float32 [2, 1024], P(None, 'tensor')
- output_weight_gradient: float32 [1024, 1024], P('tensor', 'dp')
- output_bias_gradient: float32 [1024], replicated
- second_gain_gradient: float32 [1024], replicated
- second_bias_gradient: float32 [1024], replicated
- expand_weight_gradient: float32 [2, 1024, 2736], P(None, 'dp', 'tensor')
- expand_bias_gradient: float32 [2, 2736], P(None, 'tensor')
- inner_gain_gradient: float32 [2736], P('tensor')
- inner_bias_gradient: float32 [2736], P('tensor')
- shrink_weight_gradient: float32 [2736, 1024], P('tensor', 'dp')
- shrink_bias_gradient: float32 [1024], replicated
Inputs may be any that keep to these rules, and one draw needn't show every extreme that they name: `image_valid`: 1 for an image slot in use, 0 for an empty one. `key_mask`: 1 where a position takes part as a key; 1 at position 0, 0 at positions 1025 and beyond. `patch_rows`: with patch_cols, positions 1 to 1024 of an image name every cell of the 32 x 32 grid once; 0 at position 0 and at positions 1025 and beyond. `patch_cols`: with patch_rows, positions 1 to 1024 of an image name every cell of the 32 x 32 grid once; 0 at position 0 and at positions 1025 and beyond.
All inputs are finite; a program needn't handle non-finite values.
Results may differ from a plain program's by a relative error of at most 0.015.
Values may be sent and summed in bfloat16 or wider, within the bound.
A program may use at most 192 MiB of HBM per device.

v0:
```python
import math

import jax
import jax.numpy as jnp
from jax import lax
from jax.sharding import PartitionSpec as P

DH = 64
FF_REAL = 2730
LEN = 1025


norm_eps = 1e-06
masked_score = -1e30


def row_norm(values):
    centre = values - jnp.mean(values, -1, keepdims=True)
    scale = lax.rsqrt(jnp.mean(centre * centre, -1, keepdims=True) + norm_eps)
    return (centre * scale, scale)


def norm_back(upstream, hatted, scale, gain):
    scaled = upstream * gain
    return scale * (
        scaled
        - jnp.mean(scaled, -1, keepdims=True)
        - hatted * jnp.mean(scaled * hatted, -1, keepdims=True)
    )


def swap_pairs(values):
    even_cols = jnp.arange(values.shape[-1]) % 2 == 0
    return jnp.where(even_cols, -jnp.roll(values, -1, -1), jnp.roll(values, 1, -1))


def turn_tables(row_index, col_index, columns):
    within = jnp.arange(columns) % DH
    pair_num = within // 2
    quarter = DH // 4
    freq_num = jnp.exp(-math.log(10000.0) * (pair_num % quarter).astype(jnp.float32) / quarter)
    position = jnp.where(pair_num < quarter, row_index[..., None], col_index[..., None]).astype(
        jnp.float32
    )
    angle = position * freq_num
    return (jnp.cos(angle), jnp.sin(angle))


def rotate(values, cos_t, sin_t):
    return values * cos_t + swap_pairs(values) * sin_t


def rotate_back(values, cos_t, sin_t):
    return values * cos_t - swap_pairs(values) * sin_t


def block_scores(query_block, key_rows, key_ok):
    scores = (
        jnp.einsum("pihc,kihc->ihpk", query_block, key_rows, preferred_element_type=jnp.float32)
        * 0.125
    )
    return jnp.where(key_ok, scores, masked_score)


def on_device(
    tokens,
    cotangent,
    image_valid,
    key_mask,
    patch_rows,
    patch_cols,
    first_gain,
    first_bias,
    input_weight,
    input_bias,
    output_weight,
    output_bias,
    second_gain,
    second_bias,
    expand_weight,
    expand_bias,
    inner_gain,
    inner_bias,
    shrink_weight,
    shrink_bias,
):
    tensor_size = lax.axis_size("tensor")
    tensor_rank = lax.axis_index("tensor")
    local_rows, images, model_width = tokens.shape
    seq_len = local_rows * tensor_size
    head_cols = input_weight.shape[2]
    head_count = head_cols // DH
    hidden_cols = expand_weight.shape[2]
    total_rows = seq_len * images
    gathered = (
        lax.all_gather(input_weight, "dp", axis=1, tiled=True),
        lax.all_gather(output_weight, "dp", axis=1, tiled=True),
        lax.all_gather(expand_weight, "dp", axis=1, tiled=True),
        lax.all_gather(shrink_weight, "dp", axis=1, tiled=True),
    )
    input_full, output_full, expand_full, shrink_full = gathered
    tokens_wide = tokens.astype(jnp.float32)
    tokens_hat, tokens_scale = row_norm(tokens_wide)
    norm_one = (tokens_hat * first_gain + first_bias).astype(jnp.bfloat16)
    rows_one = lax.all_gather(norm_one, "tensor", axis=0, tiled=True).reshape(
        total_rows, model_width
    )
    q_proj = jnp.dot(rows_one, input_full[0], preferred_element_type=jnp.float32) + input_bias[0]
    k_proj = jnp.dot(rows_one, input_full[1], preferred_element_type=jnp.float32)
    values = (
        jnp.dot(rows_one, input_full[2], preferred_element_type=jnp.float32) + input_bias[1]
    ).astype(jnp.bfloat16)
    cos_t, sin_t = turn_tables(patch_rows.T, patch_cols.T, head_cols)
    cos_t = cos_t.reshape(total_rows, head_cols)
    sin_t = sin_t.reshape(total_rows, head_cols)
    shape_four = (seq_len, images, head_count, DH)
    queries = rotate(q_proj, cos_t, sin_t).astype(jnp.bfloat16).reshape(shape_four)
    keys_low = rotate(k_proj, cos_t, sin_t).astype(jnp.bfloat16).reshape(shape_four)
    values = values.reshape(shape_four)
    key_ok = (key_mask > 0)[:, None, None, :]
    block_count = max(1, seq_len // 512)
    block_rows = seq_len // block_count
    attended_parts = []
    lse_parts = []
    for block_num in range(block_count):
        query_block = queries[block_num * block_rows : (block_num + 1) * block_rows]
        scores = block_scores(query_block, keys_low, key_ok)
        row_top = jnp.max(scores, -1, keepdims=True)
        expo_vals = jnp.exp(scores - row_top)
        row_total = jnp.sum(expo_vals, -1, keepdims=True)
        probs_low = (expo_vals / row_total).astype(jnp.bfloat16)
        attended_parts.append(
            jnp.einsum(
                "ihpk,kihc->pihc", probs_low, values, preferred_element_type=jnp.float32
            ).astype(jnp.bfloat16)
        )
        lse_parts.append(row_top + jnp.log(row_total))
    attended = jnp.concatenate(attended_parts, 0).reshape(seq_len, images, head_cols)
    count = lax.axis_size("tensor") * local_rows
    piece_rows = attended.reshape(count * images, head_cols)
    middle = (
        tokens_wide
        + lax.psum_scatter(
            jnp.dot(piece_rows, output_full, preferred_element_type=jnp.float32).reshape(
                count, images, model_width
            ),
            "tensor",
            scatter_dimension=0,
            tiled=True,
        )
        + output_bias
    )
    middle_hat, middle_scale = row_norm(middle)
    norm_two = (middle_hat * second_gain + second_bias).astype(jnp.bfloat16)
    rows_two = lax.all_gather(norm_two, "tensor", axis=0, tiled=True).reshape(
        total_rows, model_width
    )
    gate_pre = (
        jnp.dot(rows_two, expand_full[0], preferred_element_type=jnp.float32) + expand_bias[0]
    )
    up_pre = jnp.dot(rows_two, expand_full[1], preferred_element_type=jnp.float32) + expand_bias[1]
    column_ids = tensor_rank * hidden_cols + jnp.arange(hidden_cols)
    keep_cols = (column_ids < FF_REAL).astype(jnp.float32)
    hidden = jax.nn.silu(gate_pre) * up_pre * keep_cols
    inner_sums = lax.psum((jnp.sum(hidden, -1), jnp.sum(hidden * hidden, -1)), "tensor")
    inner_mean = inner_sums[0] / FF_REAL
    inner_var = inner_sums[1] / FF_REAL - inner_mean * inner_mean
    inner_scale = lax.rsqrt(inner_var + norm_eps)[:, None]
    hidden_hat = (hidden - inner_mean[:, None]) * inner_scale
    normed_hidden = ((hidden_hat * inner_gain + inner_bias) * keep_cols).astype(jnp.bfloat16)
    piece_rows = normed_hidden
    result_wide = (
        middle
        + lax.psum_scatter(
            jnp.dot(piece_rows, shrink_full, preferred_element_type=jnp.float32)
            .reshape(local_rows * lax.axis_size("tensor"), images, model_width)
            .astype(jnp.bfloat16),
            "tensor",
            scatter_dimension=0,
            tiled=True,
        ).astype(jnp.float32)
        + shrink_bias
    )
    result = result_wide.astype(jnp.bfloat16)
    position = tensor_rank * local_rows + jnp.arange(local_rows)
    row_weight = (position < LEN).astype(jnp.float32)[:, None] * image_valid.astype(jnp.float32)[
        None, :
    ]
    out_grad = cotangent.astype(jnp.float32) * row_weight[..., None]
    out_grad_low = out_grad.astype(jnp.bfloat16)
    rows_grad = lax.all_gather(out_grad_low, "tensor", axis=0, tiled=True).reshape(
        total_rows, model_width
    )
    back_weights = (
        lax.all_gather(input_weight, "dp", axis=1, tiled=True),
        lax.all_gather(output_weight, "dp", axis=1, tiled=True),
        lax.all_gather(expand_weight, "dp", axis=1, tiled=True),
        lax.all_gather(shrink_weight, "dp", axis=1, tiled=True),
    )
    input_back, output_back, expand_back, shrink_back = back_weights
    shrink_grad = jnp.einsum(
        "rf,rd->fd", normed_hidden, rows_grad, preferred_element_type=jnp.float32
    )
    shrink_bias_part = jnp.sum(out_grad_low.astype(jnp.float32), (0, 1))
    normed_grad = (
        jnp.einsum("rd,fd->rf", rows_grad, shrink_back, preferred_element_type=jnp.float32)
        * keep_cols
    )
    inner_gain_part = jnp.sum(normed_grad * hidden_hat, 0)
    inner_bias_part = jnp.sum(normed_grad, 0)
    hat_grad = normed_grad * inner_gain
    back_sums = lax.psum((jnp.sum(hat_grad, -1), jnp.sum(hat_grad * hidden_hat, -1)), "tensor")
    hidden_grad = (
        inner_scale
        * (
            hat_grad
            - back_sums[0][:, None] / FF_REAL
            - hidden_hat * back_sums[1][:, None] / FF_REAL
        )
        * keep_cols
    )
    gate_sigmoid = jax.nn.sigmoid(gate_pre)
    gate_grad = (
        hidden_grad * up_pre * gate_sigmoid * (1.0 + gate_pre * (1.0 - gate_sigmoid))
    ).astype(jnp.bfloat16)
    up_grad = (hidden_grad * (gate_pre * gate_sigmoid)).astype(jnp.bfloat16)
    expand_grad = jnp.stack(
        [
            jnp.einsum("rd,rf->df", rows_two, gate_grad, preferred_element_type=jnp.float32),
            jnp.einsum("rd,rf->df", rows_two, up_grad, preferred_element_type=jnp.float32),
        ]
    )
    expand_bias_part = jnp.stack(
        [jnp.sum(gate_grad.astype(jnp.float32), 0), jnp.sum(up_grad.astype(jnp.float32), 0)]
    )
    summed = jnp.einsum("rf,df->rd", gate_grad, expand_back[0], preferred_element_type=jnp.float32)
    summed = summed + jnp.einsum(
        "rf,df->rd", up_grad, expand_back[1], preferred_element_type=jnp.float32
    )
    norm_two_grad = lax.psum_scatter(
        summed.reshape(lax.axis_size("tensor") * local_rows, images, model_width),
        "tensor",
        scatter_dimension=0,
        tiled=True,
    )
    second_gain_part = jnp.sum(norm_two_grad * middle_hat, (0, 1))
    second_bias_part = jnp.sum(norm_two_grad, (0, 1))
    middle_grad = out_grad + norm_back(norm_two_grad, middle_hat, middle_scale, second_gain)
    middle_grad_low = middle_grad.astype(jnp.bfloat16)
    rows_middle = lax.all_gather(middle_grad_low, "tensor", axis=0, tiled=True).reshape(
        total_rows, model_width
    )
    output_grad = jnp.einsum(
        "rc,rd->cd",
        attended.reshape(total_rows, head_cols),
        rows_middle,
        preferred_element_type=jnp.float32,
    )
    output_bias_part = jnp.sum(middle_grad_low.astype(jnp.float32), (0, 1))
    attended_grad = (
        jnp.einsum("rd,cd->rc", rows_middle, output_back, preferred_element_type=jnp.float32)
        .astype(jnp.bfloat16)
        .reshape(shape_four)
    )
    key_turned = jnp.zeros(shape_four, jnp.float32)
    value_grad = jnp.zeros(shape_four, jnp.float32)
    query_parts = []
    for block_num in range(block_count):
        query_block = queries[block_num * block_rows : (block_num + 1) * block_rows]
        grad_block = attended_grad[block_num * block_rows : (block_num + 1) * block_rows]
        scores = block_scores(query_block, keys_low, key_ok)
        probs_full = jnp.exp(scores - lse_parts[block_num])
        probs_low = probs_full.astype(jnp.bfloat16)
        prob_grad = jnp.einsum(
            "pihc,kihc->ihpk", grad_block, values, preferred_element_type=jnp.float32
        )
        row_dot = jnp.sum(probs_full * prob_grad, -1, keepdims=True)
        score_grad = (probs_full * (prob_grad - row_dot)).astype(jnp.bfloat16)
        query_parts.append(
            jnp.einsum("ihpk,kihc->pihc", score_grad, keys_low, preferred_element_type=jnp.float32)
            * 0.125
        )
        key_turned = (
            key_turned
            + jnp.einsum(
                "ihpk,pihc->kihc", score_grad, query_block, preferred_element_type=jnp.float32
            )
            * 0.125
        )
        value_grad = value_grad + jnp.einsum(
            "ihpk,pihc->kihc", probs_low, grad_block, preferred_element_type=jnp.float32
        )
    query_turned = jnp.concatenate(query_parts, 0).reshape(total_rows, head_cols)
    query_low = rotate_back(query_turned, cos_t, sin_t).astype(jnp.bfloat16)
    key_low = rotate_back(key_turned.reshape(total_rows, head_cols), cos_t, sin_t).astype(
        jnp.bfloat16
    )
    value_low = value_grad.reshape(total_rows, head_cols).astype(jnp.bfloat16)
    input_grad = jnp.stack(
        [
            jnp.einsum("rd,rc->dc", rows_one, query_low, preferred_element_type=jnp.float32),
            jnp.einsum("rd,rc->dc", rows_one, key_low, preferred_element_type=jnp.float32),
            jnp.einsum("rd,rc->dc", rows_one, value_low, preferred_element_type=jnp.float32),
        ]
    )
    input_bias_part = jnp.stack(
        [jnp.sum(query_low.astype(jnp.float32), 0), jnp.sum(value_low.astype(jnp.float32), 0)]
    )
    summed = jnp.einsum("rc,dc->rd", query_low, input_back[0], preferred_element_type=jnp.float32)
    summed = summed + jnp.einsum(
        "rc,dc->rd", key_low, input_back[1], preferred_element_type=jnp.float32
    )
    summed = summed + jnp.einsum(
        "rc,dc->rd", value_low, input_back[2], preferred_element_type=jnp.float32
    )
    norm_one_grad = lax.psum_scatter(
        summed.reshape(local_rows * lax.axis_size("tensor"), images, model_width).astype(
            jnp.bfloat16
        ),
        "tensor",
        scatter_dimension=0,
        tiled=True,
    ).astype(jnp.float32)
    first_gain_part = jnp.sum(norm_one_grad * tokens_hat, (0, 1))
    first_bias_part = jnp.sum(norm_one_grad, (0, 1))
    tokens_gradient = middle_grad + norm_back(norm_one_grad, tokens_hat, tokens_scale, first_gain)
    weight_sums = (
        lax.psum_scatter(input_grad, "dp", scatter_dimension=1, tiled=True),
        lax.psum_scatter(output_grad, "dp", scatter_dimension=1, tiled=True),
        lax.psum_scatter(expand_grad, "dp", scatter_dimension=1, tiled=True),
        lax.psum_scatter(shrink_grad, "dp", scatter_dimension=1, tiled=True),
    )
    shared_parts = jnp.stack(
        [
            first_gain_part,
            first_bias_part,
            output_bias_part,
            second_gain_part,
            second_bias_part,
            shrink_bias_part,
        ]
    )
    zero_index = jnp.zeros((), jnp.int32)
    placed_heads = lax.dynamic_update_slice(
        jnp.zeros((2, head_cols * tensor_size), jnp.float32),
        input_bias_part,
        (zero_index, tensor_rank * head_cols),
    )
    hidden_parts = jnp.stack(
        [expand_bias_part[0], expand_bias_part[1], inner_gain_part, inner_bias_part]
    )
    placed_hidden = lax.dynamic_update_slice(
        jnp.zeros((4, hidden_cols * tensor_size), jnp.float32),
        hidden_parts,
        (zero_index, tensor_rank * hidden_cols),
    )
    small_sums = lax.psum((shared_parts, placed_heads, placed_hidden), ("dp", "tensor"))
    own_heads = lax.dynamic_slice_in_dim(small_sums[1], tensor_rank * head_cols, head_cols, 1)
    own_hidden = lax.dynamic_slice_in_dim(small_sums[2], tensor_rank * hidden_cols, hidden_cols, 1)
    shared_sums = small_sums[0]
    return (
        result,
        tokens_gradient,
        shared_sums[0],
        shared_sums[1],
        weight_sums[0],
        own_heads,
        weight_sums[1],
        shared_sums[2],
        shared_sums[3],
        shared_sums[4],
        weight_sums[2],
        own_hidden[0:2],
        own_hidden[2],
        own_hidden[3],
        weight_sums[3],
        shared_sums[5],
    )


def solution(mesh):
    return jax.shard_map(
        on_device,
        mesh=mesh,
        in_specs=(
            P("tensor", "dp", None),
            P("tensor", "dp", None),
            P("dp"),
            P("dp", None),
            P("dp", None),
            P("dp", None),
            P(),
            P(),
            P(None, "dp", "tensor"),
            P(None, "tensor"),
            P("tensor", "dp"),
            P(),
            P(),
            P(),
            P(None, "dp", "tensor"),
            P(None, "tensor"),
            P("tensor"),
            P("tensor"),
            P("tensor", "dp"),
            P(),
        ),
        out_specs=(
            P("tensor", "dp", None),
            P("tensor", "dp", None),
            P(),
            P(),
            P(None, "dp", "tensor"),
            P(None, "tensor"),
            P("tensor", "dp"),
            P(),
            P(),
            P(),
            P(None, "dp", "tensor"),
            P(None, "tensor"),
            P("tensor"),
            P("tensor"),
            P("tensor", "dp"),
            P(),
        ),
        check_vma=False,
    )
```

profile of v0, /device:TPU:0, one launch (start us, length us, event | category | flops | bytes accessed | tf_op | source)
XLA Modules:
  0.0 1358.6 jit_solution(5673731151797563802)
XLA Ops:
  7.2 2.5 fusion.96
  9.8 4.9 multiply_reduce_fusion.11
  14.8 2.8 add_convert_fusion.1
  18.5 12.5 all_gather.30
  31.0 70.4 %all-gather.8.cloned.1.call-done = bf16[1028,1,1024]{2,1,0:T(2,128)(2,1)} async-done(((bf16[257,1,1024]{2,1,0:T(2,128)(2,1)}), bf16[1028,1,1024]{2,1,0:T(2,128)(2,1)}) %all-gather.8.cloned.1.call-update) | async-done | bytes 2105360 | tf_op jit(solution)/shard_map/all_gather | solution.py:105
  101.4 3.0 copy.118
  104.5 23.1 %all-gather.10.cloned.1.call-done = bf16[3,1024,256]{2,1,0:T(8,128)(2,1)} async-done(((bf16[3,128,256]{2,1,0:T(8,128)(2,1)}), bf16[3,1024,256]{2,1,0:T(8,128)(2,1)}) %all-gather.10.cloned.1.call-update) | async-done | bytes 1572880 | tf_op jit(solution)/shard_map/all_gather | solution.py:96
  127.6 1.9 fusion.46
  129.6 2.3 convolution_add_fusion.4
  133.3 2.6 fusion.136
  138.8 8.4 fusion.79
  155.5 2.3 fusion.69
  159.5 2.4 fusion.68
  162.8 17.3 %copy.98 = f32[1028,1,1024]{2,1,0:T(1,128)} copy(f32[1028,1,1024]{2,0,1:T(8,128)S(1)} %convolution_bitcast_fusion) | data formatting | bytes 8421376 | tf_op jit(solution)/shard_map/reshape | solution.py:144
  182.0 154.0 %all-reduce.14.cloned.1.call-done = f32[1028,1,1024]{2,1,0:T(1,128)} async-done(((f32[1028,1,1024]{2,1,0:T(1,128)}), f32[1028,1,1024]{2,1,0:T(1,128)}) %all-reduce.14.cloned.1.call-update) | async-done | bytes 4210704
  336.0 3.4 fusion.128
  339.3 3.5 multiply_reduce_fusion.10
  342.9 2.8 add_convert_fusion
  348.8 3.5 convert_reduce_fusion.4
  355.3 70.6 %all-gather.12.cloned.1.call-done = bf16[1028,1,1024]{2,1,0:T(2,128)(2,1)} async-done(((bf16[257,1,1024]{2,1,0:T(2,128)(2,1)}), bf16[1028,1,1024]{2,1,0:T(2,128)(2,1)}) %all-gather.12.cloned.1.call-update) | async-done | bytes 2105360 | tf_op jit(solution)/shard_map/all_gather | solution.py:155
  425.9 4.3 copy.119
  430.2 27.9 %all-gather.14.cloned.1.call-done = bf16[2,1024,684]{1,2,0:T(8,128)(2,1)} async-done(((bf16[2,128,684]{1,2,0:T(8,128)(2,1)}), bf16[2,1024,684]{1,2,0:T(8,128)(2,1)}) %all-gather.14.cloned.1.call-update) | async-done | bytes 2801680 | tf_op jit(solution)/shard_map/all_gather | solution.py:98
  458.1 4.0 convolution_add_fusion.3
  462.2 5.2 fusion.124
  467.4 18.7 %all-reduce.8 = (f32[1028]{0:T(1024)S(1)}, f32[1028]{0:T(1024)S(1)}) all-reduce(f32[1028]{0:T(1024)S(1)} %get-tuple-element.89, f32[1028]{0:T(1024)S(1)} %get-tuple-element.88), channel_id=1, replica_groups=mesh['dp'=8,'tensor'=4] {'tensor'}, use_global_device_ids=true, to_apply=%region_12.13 | all-reduce | flops 2056 | bytes 16448 | tf_op jit(solution)/shard_map/psum | solution.py:165
  486.2 81.5 %all-gather.18.cloned.1.call-done = bf16[1028,1,1024]{2,1,0:T(2,128)(2,1)} async-done(((bf16[257,1,1024]{2,1,0:T(2,128)(2,1)}), bf16[1028,1,1024]{2,1,0:T(2,128)(2,1)}) %all-gather.18.cloned.1.call-update) | async-done | bytes 2105360 | tf_op jit(solution)/shard_map/all_gather | solution.py:191
  567.7 8.0 multiply_reduce_fusion.2
  575.7 16.3 %all-reduce.7 = (f32[1028]{0:T(1024)S(1)}, f32[1028]{0:T(1024)S(1)}) all-reduce(f32[1028]{0:T(1024)S(1)} %get-tuple-element.81, f32[1028]{0:T(1024)S(1)} %get-tuple-element.86), channel_id=1, replica_groups=mesh['dp'=8,'tensor'=4] {'tensor'}, use_global_device_ids=true, to_apply=%region_17.18 | all-reduce | flops 2056 | bytes 16448 | tf_op jit(solution)/shard_map/psum | solution.py:212
  592.0 6.2 convert_reduce_fusion
  601.9 16.9 %copy.102 = f32[1028,1,1024]{2,1,0:T(1,128)} copy(f32[1028,1,1024]{2,0,1:T(8,128)S(1)} %fusion.15) | data formatting | bytes 8421376 | tf_op jit(solution)/shard_map/reshape | solution.py:241
  618.9 154.2 %all-reduce.16.cloned.1.call-done = f32[1028,1,1024]{2,1,0:T(1,128)} async-done(((f32[1028,1,1024]{2,1,0:T(1,128)}), f32[1028,1,1024]{2,1,0:T(1,128)}) %all-reduce.16.cloned.1.call-update) | async-done | bytes 4210704
  773.1 6.4 multiply_reduce_fusion.6
  779.5 4.9 convert_reduce_fusion.5
  791.3 6.1 fusion.53
  797.4 3.7 fusion.50
  801.2 3.5 fusion.18
  804.7 62.6 %all-gather.20.cloned.1.call-done = bf16[1028,1,1024]{2,1,0:T(2,128)(2,1)} async-done(((bf16[257,1,1024]{2,1,0:T(2,128)(2,1)}), bf16[1028,1,1024]{2,1,0:T(2,128)(2,1)}) %all-gather.20.cloned.1.call-update) | async-done | bytes 2105360 | tf_op jit(solution)/shard_map/all_gather | solution.py:250
  867.3 3.0 convolution_convert_fusion.1
  871.4 6.1 multiply_reduce_fusion.1
  878.0 2.3 multiply_convert_fusion.1
  880.3 2.5 convolution_multiply_fusion.2
  885.8 5.9 fusion.7
  891.8 5.3 multiply_reduce_fusion
  897.1 2.1 multiply_convert_fusion
  907.6 3.7 convert_reduce_fusion.2
  917.6 2.7 copy.122
  923.5 4.8 fusion.71
  928.5 5.7 convert_reduce_fusion.3
  936.8 77.3 %fusion.125 = (bf16[264,1024]{1,0:T(8,128)(2,1)}, bf16[264,1024]{1,0:T(8,128)(2,1)}) fusion(bf16[1028,1,1024]{2,0,1:T(8,128)(2,1)} %fusion.18, bf16[1028,1,1024]{2,0,1:T(8,128)(2,1)S(1)} %fusion.17), kind=kCustom, calls=%all-reduce-scatter.2 | all-reduce-scatter fusion | flops 2162689 | bytes 5292544
  1018.0 3.0 concatenate.60
  1021.2 5.1 multiply_reduce_fusion.7
  1027.0 6.1 pad_maximum_fusion
  1033.8 7.4 fusion.31
  1041.3 4.4 fusion.28
  1046.1 2.7 fusion.62
  1053.8 4.3 collective-permute-start
  1059.8 3.7 concatenate.59
  1066.8 4.6 multiply_add_fusion
  1071.4 77.6 %all-reduce.18.cloned.1.call-done = (f32[6,1024]{1,0:T(8,128)}, f32[2,1024]{1,0:T(2,128)}, f32[4,2736]{1,0:T(4,128)}) async-done(((f32[6,1024]{1,0:T(8,128)}, f32[2,1024]{1,0:T(2,128)}, f32[4,2736]{1,0:T(4,128)}), (f32[6,1024]{1,0:T(8,128)}, f32[2,1024]{1,0:T(2,128)}, f32[4,2736]{1,0:T(4,128)})) %all-reduce.18.cloned.1.call-update) | async-done | bytes 76560 | tf_op jit(solution)/shard_map/psum | solution.py:357
  1154.7 57.8 %reduce-scatter.15.cloned.1.call-done = f32[2,128,684]{1,2,0:T(8,128)} async-done(((f32[2,1024,684]{1,2,0:T(8,128)}), f32[2,128,684]{1,2,0:T(8,128)}) %reduce-scatter.15.cloned.1.call-update) | async-done | bytes 700432 | tf_op jit(solution)/shard_map/reduce_scatter | solution.py:330
  1212.5 2.3 copy.113
  1214.8 46.9 %reduce-scatter.17.cloned.1.call-done = f32[684,128]{1,0:T(8,128)} async-done(((f32[684,1024]{1,0:T(8,128)}), f32[684,128]{1,0:T(8,128)}) %reduce-scatter.17.cloned.1.call-update) | async-done | bytes 350224 | tf_op jit(solution)/shard_map/reduce_scatter | solution.py:331
  1261.7 39.8 %reduce-scatter.13.cloned.1.call-done = f32[256,128]{1,0:T(8,128)} async-done(((f32[256,1024]{1,0:T(8,128)}), f32[256,128]{1,0:T(8,128)}) %reduce-scatter.13.cloned.1.call-update) | async-done | bytes 131088 | tf_op jit(solution)/shard_map/reduce_scatter | solution.py:329
  1301.5 50.1 %reduce-scatter.11.cloned.1.call-done = f32[3,128,256]{2,1,0:T(8,128)} async-done(((f32[3,1024,256]{2,1,0:T(8,128)}), f32[3,128,256]{2,1,0:T(8,128)}) %reduce-scatter.11.cloned.1.call-update) | async-done | bytes 393232 | tf_op jit(solution)/shard_map/reduce_scatter | solution.py:328
  (342 shorter events, 78.7 us)
Async XLA Ops:
  7.2 7.5 copy-start.58
  7.2 7.5 copy-start.80
  7.2 94.2 %all-gather.8.cloned.1.call-start = ((), (), s32[]{:S(2)}) async-start(), calls=%async_computation.4 | async-start | bytes 5263360 | tf_op jit(solution)/shard_map/all_gather | solution.py:105
  14.8 16.3 %copy-start.89 = (f32[2,256]{1,0:T(2,128)S(1)}, f32[2,256]{1,0:T(2,128)}, u32[]{:S(2)}) copy-start(f32[2,256]{1,0:T(2,128)} %param.29) | copy-start | bytes 6148
  17.6 110.0 %all-gather.10.cloned.1.call-start = ((), (), s32[]{:S(2)}) async-start(), calls=%async_computation.5 | async-start | bytes 1769472 | tf_op jit(solution)/shard_map/all_gather | solution.py:96
  18.3 317.7 %all-reduce.14.cloned.1.call-start = ((), (), s32[]{:S(2)}) async-start(), calls=%async_computation.15 | async-start | bytes 8421376
  18.4 120.4 %copy-start.52 = (s32[1028]{0:T(1024)}, s32[1028]{0:T(1024)S(1)}, u32[]{:S(2)}) copy-start(s32[1028]{0:T(1024)S(1)} %reduce.24) | copy-start | bytes 12340
  18.4 120.3 %copy-start.54 = (s32[1028]{0:T(1024)}, s32[1028]{0:T(1024)S(1)}, u32[]{:S(2)}) copy-start(s32[1028]{0:T(1024)S(1)} %reduce.25) | copy-start | bytes 12340
  104.4 25.1 %copy-start.39 = (bf16[1028,1,1024]{2,0,1:T(8,128)(2,1)}, bf16[1028,1,1024]{2,0,1:T(8,128)(2,1)S(1)}, u32[]{:S(2)}) copy-start(bf16[1028,1,1024]{2,0,1:T(8,128)(2,1)S(1)} %copy.118) | copy-start | bytes 6316036
  138.8 732.6 %copy-start.11 = (bf16[1028,256]{0,1:T(8,128)(2,1)}, bf16[1028,256]{0,1:T(8,128)(2,1)S(1)}, u32[]{:S(2)}) copy-start(bf16[1028,256]{0,1:T(8,128)(2,1)S(1)} %copy.94) | copy-start | bytes 1579012
  153.7 5.8 copy-start
  180.1 155.9 %copy-start.13 = (bf16[257,1,1024]{2,0,1:T(8,128)(2,1)S(1)}, bf16[257,1,1024]{2,0,1:T(8,128)(2,1)}, u32[]{:S(2)}) copy-start(bf16[257,1,1024]{2,0,1:T(8,128)(2,1)} %param.20) | copy-start | bytes 1579012
  180.1 155.9 %copy-start.81 = (f32[1024]{0:T(1024)S(1)}, f32[1024]{0:T(1024)}, u32[]{:S(2)}) copy-start(f32[1024]{0:T(1024)} %param.31) | copy-start | bytes 12292
  180.1 162.8 %copy-start.57 = (f32[1024]{0:T(1024)S(1)}, f32[1024]{0:T(1024)}, u32[]{:S(2)}) copy-start(f32[1024]{0:T(1024)} %param.32) | copy-start | bytes 12292
  180.1 162.8 %copy-start.82 = (f32[1024]{0:T(1024)S(1)}, f32[1024]{0:T(1024)}, u32[]{:S(2)}) copy-start(f32[1024]{0:T(1024)} %param.33) | copy-start | bytes 12292
  180.1 245.8 %all-gather.12.cloned.1.call-start = ((), (), s32[]{:S(2)}) async-start(), calls=%async_computation.6 | async-start | bytes 5263360 | tf_op jit(solution)/shard_map/all_gather | solution.py:155
  345.7 112.4 %all-gather.14.cloned.1.call-start = ((), (), s32[]{:S(2)}) async-start(), calls=%async_computation.7 | async-start | bytes 3170304 | tf_op jit(solution)/shard_map/all_gather | solution.py:98
  347.5 138.6 %all-gather.16.cloned.1.call-start = ((), (), s32[]{:S(2)}) async-start(), calls=%async_computation.8 | async-start | bytes 1585152 | tf_op jit(solution)/shard_map/all_gather | solution.py:99
  348.1 219.6 %all-gather.18.cloned.1.call-start = ((), (), s32[]{:S(2)}) async-start(), calls=%async_computation.9 | async-start | bytes 5263360 | tf_op jit(solution)/shard_map/all_gather | solution.py:191
  348.8 6.4 copy-start.76
  355.0 418.0 %all-reduce.16.cloned.1.call-start = ((), (), s32[]{:S(2)}) async-start(), calls=%async_computation.16 | async-start | bytes 8421376
  355.3 445.9 %copy-start.73 = (f32[684]{0:T(1024)}, f32[684]{0:T(1024)S(1)}, u32[]{:S(2)}) copy-start(f32[684]{0:T(1024)S(1)} %fusion.101) | copy-start | bytes 8212
  462.1 5.3 copy-start.26
  462.2 105.5 %copy-start.83 = (f32[684]{0:T(1024)S(1)}, f32[684]{0:T(1024)}, u32[]{:S(2)}) copy-start(f32[684]{0:T(1024)} %param.36) | copy-start | bytes 8212
  486.1 315.0 %copy-start.60 = (f32[1028]{0:T(1024)}, f32[1028]{0:T(1024)S(1)}, u32[]{:S(2)}) copy-start(f32[1028]{0:T(1024)S(1)} %get-tuple-element.160) | copy-start | bytes 12340
  486.1 315.0 %copy-start.62 = (f32[1028]{0:T(1024)}, f32[1028]{0:T(1024)S(1)}, u32[]{:S(2)}) copy-start(f32[1028]{0:T(1024)S(1)} %get-tuple-element.161) | copy-start | bytes 12340
  592.0 6.2 copy-start.94
  618.8 248.5 %all-gather.20.cloned.1.call-start = ((), (), s32[]{:S(2)}) async-start(), calls=%async_computation.10 | async-start | bytes 5263360 | tf_op jit(solution)/shard_map/all_gather | solution.py:250
  773.1 6.4 copy-start.3
  787.1 361.9 %all-reduce.18.cloned.1.call-start = ((), (), s32[]{:S(2)}) async-start(), calls=%async_computation.17 | async-start | bytes 172032 | tf_op jit(solution)/shard_map/psum | solution.py:357
  791.2 6.2 copy-start.51
  791.2 6.2 copy-start.43
  791.2 6.2 copy-start.47
  801.2 66.2 %copy-start.45 = (bf16[256,1024]{1,0:T(8,128)(2,1)S(1)}, bf16[256,1024]{1,0:T(8,128)(2,1)}, u32[]{:S(2)}) copy-start(bf16[256,1024]{1,0:T(8,128)(2,1)} %all_gather.30) | copy-start | bytes 1572868
  871.3 6.2 copy-start.29
  871.3 6.2 slice-start
  871.3 6.3 slice-start.1
  871.4 6.6 slice-start.2
  885.8 6.0 copy-start.12
  885.8 6.0 copy-start.31
  885.8 11.3 slice-start.6
  885.8 11.3 slice-start.7
  891.8 5.3 slice-start.8
  911.3 5.3 copy-start.10
  923.3 5.1 copy-start.38
  923.4 5.0 copy-start.20
  923.4 5.0 copy-start.21
  928.4 6.7 copy-start.18
  928.5 5.8 copy-start.16
  928.5 5.8 copy-start.50
  1014.0 7.2 copy-start.6
  1014.0 7.2 copy-start.59
  1014.0 12.3 copy-start.69
  1014.0 12.3 copy-start.70
  1014.0 12.3 copy-start.71
  1014.0 12.3 copy-start.72
  1014.9 3.0 collective-permute-start.1
  1016.3 10.7 copy-start.64
  1027.0 185.5 %reduce-scatter.15.cloned.1.call-start = ((), (), s32[]{:S(2)}) async-start(), calls=%async_computation.13 | async-start | bytes 6340608 | tf_op jit(solution)/shard_map/reduce_scatter | solution.py:330
  1033.1 228.6 %reduce-scatter.17.cloned.1.call-start = ((), (), s32[]{:S(2)}) async-start(), calls=%async_computation.14 | async-start | bytes 3170304 | tf_op jit(solution)/shard_map/reduce_scatter | solution.py:331
  1041.3 260.3 %reduce-scatter.13.cloned.1.call-start = ((), (), s32[]{:S(2)}) async-start(), calls=%async_computation.12 | async-start | bytes 1179648 | tf_op jit(solution)/shard_map/reduce_scatter | solution.py:329
  1045.7 305.9 %reduce-scatter.11.cloned.1.call-start = ((), (), s32[]{:S(2)}) async-start(), calls=%async_computation.11 | async-start | bytes 3538944 | tf_op jit(solution)/shard_map/reduce_scatter | solution.py:328
  1052.7 11.9 copy-start.85
  1053.8 6.0 collective-permute-start
  (59 other events, 158.3 us)
Sparse Core Ops, SparseCore 0:
  17.7 83.7 all-gather.7
  103.3 24.2 all-gather.9
  180.2 155.6 all-reduce.13
  345.8 80.0 all-gather.11
  428.2 29.8 all-gather.13
  459.9 25.1 all-gather.15
  486.6 81.0 all-gather.17
  619.0 154.0 all-reduce.15
  787.2 80.0 all-gather.19
  1027.1 121.8 all-reduce.17
  1152.5 59.9 reduce-scatter.14
  1216.4 45.2 reduce-scatter.16
  1265.5 36.0 reduce-scatter.12
  1305.3 46.2 reduce-scatter.10
where the time goes:
time: 1370 us; the launch traced here: 1360 us
  waiting for transfers between devices  921 us (67%)
  blocking collectives  125 us (9%)
  matrix products  98.4 us (7%)
  local copies, waits for them, and re-layouts  94.9 us (7%)
  other arithmetic  94.2 us (7%)
  between operations  17.9 us (1%)
    unnamed x18, waiting for transfers between devices  313 us
    all_gather x1, waiting for transfers between devices, on_device(): lax.all_gather(out_grad_low, 'tensor', axis=0, tiled=True)  81.5 us
    psum x1, waiting for transfers between devices, on_device(): lax.psum((shared_parts, placed_heads, placed_hidden), ('dp', 'tensor'))  77.6 us
    unnamed x1, blocking collectives  77.3 us
    all_gather x1, waiting for transfers between devices, on_device(): lax.all_gather(norm_two, 'tensor', axis=0, tiled=True)  70.6 us
    all_gather x1, waiting for transfers between devices, on_device(): lax.all_gather(norm_one, 'tensor', axis=0, tiled=True)  70.4 us
    all_gather x1, waiting for transfers between devices, on_device(): lax.all_gather(middle_grad_low, 'tensor', axis=0, tiled=True)  62.6 us
    reduce_scatter x1, waiting for transfers between devices, on_device(): lax.psum_scatter(expand_grad, 'dp', scatter_dimension=1, tiled=True)  57.8 us
  transfers between devices with their start and end apart: 16, of which 15 were waited for; matrix products, arithmetic and copies ran while one was open for 6% of the time, Pallas kernels for 0%

commit v1 on v0

--- a/solution.py
+++ b/solution.py
@@ -1,8 +1,11 @@
+import functools
 import math
 
 import jax
 import jax.numpy as jnp
 from jax import lax
+from jax.experimental import pallas as pl
+from jax.experimental.pallas import tpu as pltpu
 from jax.sharding import PartitionSpec as P
 
 DH = 64
@@ -378,9 +381,1346 @@
     )
 
 
+MESH_ID = pl.DeviceIdType.MESH
+LOG2E = 1.4426950408889634
+
+
+def round_up(size, step):
+    return (size + step - 1) // step * step
+
+
+class Plan:
+    def __init__(self, local_rows, width, head_cols, hidden_cols, tensor_size):
+        self.rows = round_up(local_rows, 16)
+        self.local_rows = local_rows
+        self.width = width
+        self.head_cols = head_cols
+        self.heads = head_cols // DH
+        self.hidden = round_up(hidden_cols, 16)
+        self.hidden_cols = hidden_cols
+        self.groups = tensor_size
+        self.seq = self.rows * tensor_size
+        self.in_rows = 3 * head_cols
+        self.pack = self.in_rows + 3 * self.hidden + head_cols
+
+
+def places():
+    dp = lax.axis_index("dp")
+    core = lax.rem(dp, 2)
+    x_pos = lax.rem(dp // 2, 2)
+    y_pos = dp // 4
+    sib = dp + 1 - 2 * core
+    x_nbr = dp + 2 - 4 * x_pos
+    y_nbr = dp + 4 - 8 * y_pos
+    diag = x_nbr + 4 - 8 * y_pos
+    return dp, core, x_pos, y_pos, sib, x_nbr, y_nbr, diag
+
+
+def rcopy(src, dst, send_sem, recv_sem, dp, z):
+    return pltpu.make_async_remote_copy(
+        src_ref=src,
+        dst_ref=dst,
+        send_sem=send_sem,
+        recv_sem=recv_sem,
+        device_id=(dp, z),
+        device_id_type=MESH_ID,
+    )
+
+
+def greet(targets):
+    bar = pltpu.get_barrier_semaphore()
+    for dp, z in targets:
+        pl.semaphore_signal(bar, 1, device_id=(dp, z), device_id_type=MESH_ID)
+    pl.semaphore_wait(bar, len(targets))
+
+
+def nt_dot(left, right):
+    return lax.dot_general(
+        left, right, (((1,), (1,)), ((), ())), preferred_element_type=jnp.float32
+    )
+
+
+def nn_dot(left, right):
+    return jnp.dot(left, right, preferred_element_type=jnp.float32)
+
+
+def tn_dot(left, right):
+    return lax.dot_general(
+        left, right, (((0,), (0,)), ((), ())), preferred_element_type=jnp.float32
+    )
+
+
+def lane_swap(values):
+    cols = values.shape[1]
+    even = lax.broadcasted_iota(jnp.int32, values.shape, 1) % 2 == 0
+    return jnp.where(even, pltpu.roll(values, cols - 1, 1), pltpu.roll(values, 1, 1))
+
+
+def twice(table, cols):
+    return jnp.concatenate([table] * (cols // table.shape[1]), axis=1)
+
+
+def forward_kernel(
+    plan,
+    tok,
+    gain,
+    shift,
+    wpk,
+    sml,
+    cos_t,
+    sin_t,
+    kbias,
+    qvb,
+    g_out,
+    att_out,
+    xg,
+    qh,
+    kh,
+    vh,
+    lse,
+    sml_out,
+    obuf,
+    wv,
+    ohead,
+    tok_s,
+    tok_r,
+    sml_s,
+    sml_r,
+    att_s,
+    att_r,
+    quick_s,
+    quick_r,
+    w_s,
+    w_r,
+    loc,
+):
+    rows, heads = plan.rows, plan.heads
+    hc = plan.head_cols
+    dp, core, x_pos, y_pos, sib, x_nbr, y_nbr, diag = places()
+    z = lax.axis_index("tensor")
+    groups = plan.groups
+
+    def lanes(which):
+        return pl.ds(pl.multiple_of(which * 128, 128), 128)
+
+    def region(z_of, which, start, size):
+        return g_out.at[z_of, pl.ds(start, size), lanes(which)]
+
+    def ring(r):
+        return lax.rem(z + r, groups)
+
+    partners = [(sib, z), (x_nbr, z), (y_nbr, z), (diag, z)]
+    partners += [(dp, ring(r)) for r in range(1, groups)]
+    greet(partners)
+
+    pack, quick = plan.pack, plan.in_rows
+    offsets = []
+    for step in range(1, groups):
+        offsets += [step, -step]
+
+    def there(offset):
+        return (z + offset >= 0) & (z + offset < groups)
+
+    def when(cond, body):
+        pl.when(cond)(body)
+
+    own_copy = pltpu.make_async_copy(wpk, region(z, dp, 0, pack), loc.at[0])
+    own_copy.start()
+    for num, target in enumerate((x_nbr, y_nbr, diag, sib)):
+        rcopy(
+            wpk.at[pl.ds(0, quick)],
+            region(z, dp, 0, quick),
+            quick_s.at[num],
+            quick_r.at[num],
+            target,
+            z,
+        ).start()
+    for r in range(1, groups):
+        rcopy(sml, sml_out.at[z], sml_s.at[r], sml_r.at[r], dp, ring(r)).start()
+    sml_out[z] = sml[...]
+
+    wide = tok[...].astype(jnp.float32)
+    centre = wide - jnp.mean(wide, -1, keepdims=True)
+    scale = lax.rsqrt(jnp.mean(centre * centre, -1, keepdims=True) + norm_eps)
+    xg[z] = (centre * scale * gain[...] + shift[...]).astype(jnp.bfloat16)
+
+    def tok_send(z_of, way, num):
+        return rcopy(xg.at[z_of], xg.at[z_of], tok_s.at[z_of, num], tok_r.at[z_of], dp, z + way)
+
+    for num, way in enumerate((1, -1)):
+        when(there(way), lambda way=way, num=num: tok_send(z, way, num).start())
+
+    def w_copy(z_of, which, start, size, num, target, target_z, source=None):
+        dst = region(z_of, which, start, size)
+        return rcopy(
+            dst if source is None else source.at[pl.ds(start, size)],
+            dst,
+            w_s.at[z_of, num],
+            w_r.at[z_of, num],
+            target,
+            target_z,
+        )
+
+    def halves(offset):
+        start = quick if offset == 0 else 0
+        size = pack - start
+        first = round_up(size // 2, 16)
+        return (start, first), (start + first, size - first)
+
+    def xy_start(offset):
+        z_of = z + offset
+        (a0, an), (b0, bn) = halves(offset)
+        source = wpk if offset == 0 else None
+        w_copy(z_of, dp, a0, an, 1, x_nbr, z, source).start()
+        w_copy(z_of, dp, b0, bn, 4, y_nbr, z, source).start()
+        w_copy(z_of, dp, b0, bn, 2, x_nbr, z, source).start()
+        w_copy(z_of, dp, a0, an, 3, y_nbr, z, source).start()
+        start, size = a0, an + bn
+        w_copy(z_of, dp, start, size, 7, sib, z, source).start()
+
+    def xy_pass(offset):
+        z_of = z + offset
+        (a0, an), (b0, bn) = halves(offset)
+        w_copy(z_of, x_nbr, a0, an, 1, x_nbr, z).wait_recv()
+        w_copy(z_of, x_nbr, a0, an, 5, y_nbr, z).start()
+        w_copy(z_of, y_nbr, b0, bn, 4, y_nbr, z).wait_recv()
+        w_copy(z_of, y_nbr, b0, bn, 6, x_nbr, z).start()
+
+    def sib_pass(offset):
+        z_of = z + offset
+        (a0, an), (b0, bn) = halves(offset)
+        start, size = a0, an + bn
+        w_copy(z_of, x_nbr, b0, bn, 2, x_nbr, z).wait_recv()
+        w_copy(z_of, x_nbr, start, size, 8, sib, z).start()
+        w_copy(z_of, y_nbr, a0, an, 3, y_nbr, z).wait_recv()
+        w_copy(z_of, y_nbr, start, size, 9, sib, z).start()
+        w_copy(z_of, diag, a0, an, 5, y_nbr, z).wait_recv()
+        w_copy(z_of, diag, b0, bn, 6, x_nbr, z).wait_recv()
+        w_copy(z_of, diag, start, size, 10, sib, z).start()
+
+    def w_finish(offset):
+        z_of = z + offset
+        (a0, an), (b0, bn) = halves(offset)
+        start, size = a0, an + bn
+        for num in (7, 8, 9, 10):
+            w_copy(z_of, sib, start, size, num, sib, z).wait_recv()
+            w_copy(z_of, dp, start, size, num, sib, z).wait_send()
+        for num, (s0, sn) in ((1, (a0, an)), (2, (b0, bn)), (3, (a0, an)), (4, (b0, bn))):
+            w_copy(z_of, dp, s0, sn, num, x_nbr, z).wait_send()
+        w_copy(z_of, dp, a0, an, 5, y_nbr, z).wait_send()
+        w_copy(z_of, dp, b0, bn, 6, x_nbr, z).wait_send()
+
+    def onward(offset):
+        return -1 if offset > 0 else 1
+
+    def z_arrive(offset):
+        z_of = z + offset
+        way = onward(offset)
+        w_copy(z_of, dp, 0, pack, 0, dp, z - way).wait_recv()
+        when(there(way), lambda: w_copy(z_of, dp, 0, pack, 0, dp, z + way).start())
+        xy_start(offset)
+
+    def z_sent(offset):
+        way = onward(offset)
+        when(there(way), lambda: w_copy(z + offset, dp, 0, pack, 0, dp, z + way).wait_send())
+
+    def own_z(way, num):
+        return rcopy(
+            wpk, region(z, dp, 0, pack), w_s.at[z, num], w_r.at[z, 0], dp, z + way
+        )
+
+    for num, way in ((0, 1), (11, -1)):
+        when(there(way), lambda way=way, num=num: own_z(way, num).start())
+    xy_start(0)
+
+    def project(slot):
+        block = xg[slot]
+        place = pl.ds(pl.multiple_of(slot * rows, 16), rows)
+        cos_b = twice(cos_t[place, :], hc)
+        sin_b = twice(sin_t[place, :], hc)
+        wide_q = nt_dot(block, wv[0:hc, :]) + qvb[0:1, :]
+        q_low = (wide_q * cos_b + lane_swap(wide_q) * sin_b).astype(jnp.bfloat16)
+        wide_k = nt_dot(block, wv[hc : 2 * hc, :])
+        k_low = (wide_k * cos_b + lane_swap(wide_k) * sin_b).astype(jnp.bfloat16)
+        v_low = (nt_dot(block, wv[2 * hc : 3 * hc, :]) + qvb[1:2, :]).astype(jnp.bfloat16)
+        for head in range(heads):
+            cut = slice(head * DH, (head + 1) * DH)
+            qh[head, place, :] = q_low[:, cut]
+            kh[head, place, :] = k_low[:, cut]
+            vh[head, place, :] = v_low[:, cut]
+
+    for num, source in enumerate((x_nbr, y_nbr, diag)):
+        rcopy(
+            wpk.at[pl.ds(0, quick)],
+            region(z, source, 0, quick),
+            quick_s.at[num],
+            quick_r.at[num],
+            source,
+            z,
+        ).wait_recv()
+        there_too = region(z, source, 0, quick)
+        rcopy(there_too, there_too, quick_s.at[4 + num], quick_r.at[4 + num], sib, z).start()
+    for num in range(4):
+        rcopy(
+            wpk.at[pl.ds(0, quick)],
+            region(z, sib, 0, quick),
+            quick_s.at[3 + num],
+            quick_r.at[3 + num],
+            sib,
+            z,
+        ).wait_recv()
+    own_copy.wait()
+    fetch = pltpu.make_async_copy(g_out.at[z, pl.ds(0, quick), :], wv, loc.at[1])
+    fetch.start()
+    fetch.wait()
+    project(z)
+
+    def tok_step(offset):
+        z_of = z + offset
+        way = onward(offset)
+        tok_send(z_of, -way, 0).wait_recv()
+        when(there(way), lambda: tok_send(z_of, way, 0).start())
+        project(z_of)
+
+    when(there(1), lambda: tok_step(1))
+    when(there(-1), lambda: tok_step(-1))
+    xy_pass(0)
+    when(there(1), lambda: z_arrive(1))
+    when(there(-1), lambda: z_arrive(-1))
+    when(there(2), lambda: tok_step(2))
+    when(there(-2), lambda: tok_step(-2))
+    sib_pass(0)
+    when(there(3), lambda: tok_step(3))
+    when(there(-3), lambda: tok_step(-3))
+
+    def attend(r):
+        slot = ring(r)
+        place = pl.ds(pl.multiple_of(slot * rows, 16), rows)
+
+        @pl.loop(0, heads)
+        def _(head):
+            scores = nt_dot(qh[head, place, :], kh[head]) * (0.125 * LOG2E) + kbias[...]
+            top = jnp.max(scores, -1, keepdims=True)
+            expo = jnp.exp2(scores - top)
+            total = jnp.sum(expo, -1, keepdims=True)
+            mixed = nn_dot(expo.astype(jnp.bfloat16), vh[head])
+            ohead[head] = (mixed / total).astype(jnp.bfloat16)
+            lse[head, place, :] = top + jnp.log2(total)
+
+        joined = jnp.concatenate([ohead[head] for head in range(heads)], axis=1)
+        obuf[slot] = joined
+        if r == 0:
+            att_out[:, pl.ds(pl.multiple_of(z * hc, 128), hc)] = joined
+        else:
+            att_copy(r).start()
+
+    def att_copy(r, owner=None):
+        here = z if owner is None else owner
+        return rcopy(
+            obuf.at[ring(r)],
+            att_out.at[:, pl.ds(pl.multiple_of(here * hc, 128), hc)],
+            att_s.at[r],
+            att_r.at[r],
+            dp,
+            ring(r),
+        )
+
+    def both(offset, body):
+        when(there(offset), lambda: body(offset))
+        when(there(-offset), lambda: body(-offset))
+
+    attend(2)
+    both(1, xy_pass)
+    both(2, z_arrive)
+    attend(1)
+    both(1, sib_pass)
+    both(3, z_arrive)
+    attend(3)
+    both(2, xy_pass)
+    attend(0)
+    both(2, sib_pass)
+    both(3, xy_pass)
+    both(3, sib_pass)
+
+    for num, way in enumerate((1, -1)):
+        when(there(way), lambda way=way, num=num: tok_send(z, way, num).wait_send())
+    for num, way in ((0, 1), (11, -1)):
+        when(there(way), lambda way=way, num=num: own_z(way, num).wait_send())
+    for offset in offsets:
+
+        def sent(offset=offset):
+            way = onward(offset)
+            when(there(way), lambda: tok_send(z + offset, way, 0).wait_send())
+            z_sent(offset)
+            w_finish(offset)
+
+        when(there(offset), sent)
+    w_finish(0)
+    for num in range(7):
+        rcopy(
+            wpk.at[pl.ds(0, quick)],
+            region(z, dp, 0, quick),
+            quick_s.at[num],
+            quick_r.at[num],
+            sib,
+            z,
+        ).wait_send()
+    for r in range(1, groups):
+        back = lax.rem(z + groups - r, groups)
+        sml_copy = rcopy(sml, sml_out.at[back], sml_s.at[r], sml_r.at[r], dp, ring(r))
+        sml_copy.wait_recv()
+        sml_copy.wait_send()
+        att_copy(r, back).wait_recv()
+        att_copy(r).wait_send()
+
+
+def forward_call(plan, *operands):
+    rows, seq, heads, groups = plan.rows, plan.seq, plan.heads, plan.groups
+    low, wide = jnp.bfloat16, jnp.float32
+    vmem = pl.BlockSpec(memory_space=pltpu.VMEM)
+    any_space = pl.BlockSpec(memory_space=pl.ANY)
+    dma = pltpu.SemaphoreType.DMA
+    return pl.pallas_call(
+        functools.partial(forward_kernel, plan),
+        out_shape=(
+            jax.ShapeDtypeStruct((groups, plan.pack, plan.width), low),
+            jax.ShapeDtypeStruct((rows, plan.width), low),
+            jax.ShapeDtypeStruct((groups, rows, plan.width), low),
+            jax.ShapeDtypeStruct((heads, seq, DH), low),
+            jax.ShapeDtypeStruct((heads, seq, DH), low),
+            jax.ShapeDtypeStruct((heads, seq, DH), low),
+            jax.ShapeDtypeStruct((heads, seq, 1), wide),
+            jax.ShapeDtypeStruct((groups,) + operands[4].shape, wide),
+            jax.ShapeDtypeStruct((groups, rows, plan.head_cols), low),
+        ),
+        in_specs=[vmem, vmem, vmem, any_space, vmem, vmem, vmem, vmem, vmem],
+        out_specs=(any_space,) + (vmem,) * 8,
+        scratch_shapes=[
+            pltpu.VMEM((plan.in_rows, plan.width), low),
+            pltpu.VMEM((heads, rows, DH), low),
+            dma((groups, 2)),
+            dma((groups,)),
+            dma((groups,)),
+            dma((groups,)),
+            dma((groups,)),
+            dma((groups,)),
+            dma((7,)),
+            dma((7,)),
+            dma((groups, 12)),
+            dma((groups, 12)),
+            dma((2,)),
+        ],
+        compiler_params=pltpu.CompilerParams(
+            collective_id=0, has_side_effects=True, vmem_limit_bytes=56 * 2**20
+        ),
+        name="gather_attend",
+    )(*operands)
+
+
+def pad_rows(array, count):
+    return jnp.pad(array, ((0, count - array.shape[0]),) + ((0, 0),) * (array.ndim - 1))
+
+
+def by_group(table, plan):
+    split = table.reshape(plan.groups, plan.local_rows)
+    return jnp.pad(split, ((0, 0), (0, plan.rows - plan.local_rows)))
+
+
+def rotation_tables(patch_rows, patch_cols, plan, columns):
+    channel = jnp.arange(columns) % DH
+    pair = channel // 2
+    quarter = DH // 4
+    freq = jnp.exp(-math.log(10000.0) * (pair % quarter).astype(jnp.float32) / quarter)
+    row_at = by_group(patch_rows, plan).reshape(-1, 1)
+    col_at = by_group(patch_cols, plan).reshape(-1, 1)
+    angle = jnp.where(pair < quarter, row_at, col_at).astype(jnp.float32) * freq
+    sign = jnp.where(channel % 2 == 0, -1.0, 1.0)
+    return jnp.cos(angle), jnp.sin(angle) * sign
+
+
+def pack_weights(input_weight, output_weight, expand_weight, shrink_weight, plan):
+    extra = plan.hidden - plan.hidden_cols
+    flipped_in = jnp.swapaxes(input_weight, 1, 2).reshape(plan.in_rows, -1)
+    flipped = jnp.pad(jnp.swapaxes(expand_weight, 1, 2), ((0, 0), (0, extra), (0, 0)))
+    flipped = flipped.reshape(2 * plan.hidden, -1)
+    return jnp.concatenate(
+        [flipped_in, flipped, pad_rows(shrink_weight, plan.hidden), output_weight], axis=0
+    )
+
+
+def hidden_vectors(expand_bias, inner_gain, inner_bias, plan):
+    stacked = jnp.concatenate([expand_bias, inner_gain[None], inner_bias[None]], axis=0)
+    lanes = round_up(plan.hidden, 128)
+    return jnp.pad(stacked, ((0, 4), (0, lanes - plan.hidden_cols)))
+
+
+def block_kernel(
+    plan,
+    tok,
+    att,
+    cot,
+    row_weight,
+    vectors,
+    hid_vec,
+    g_in,
+    result,
+    mid_grad,
+    att_grad,
+    regroup,
+    normed,
+    gate_g,
+    up_g,
+    small_a,
+    small_h,
+    x_two,
+    og_low,
+    w_ff,
+    w_out,
+    gate_s,
+    up_s,
+    hat_s,
+    grad_s,
+    acc,
+    load,
+):
+    groups, hc, hid = plan.groups, plan.head_cols, plan.hidden
+    ff_start, out_start = plan.in_rows, plan.pack - hc
+    for num in range(groups):
+        pltpu.make_async_copy(
+            g_in.at[num, pl.ds(out_start, hc), :], w_out.at[num], load.at[0, num]
+        ).start()
+    for num in range(groups):
+        pltpu.make_async_copy(
+            g_in.at[num, pl.ds(ff_start, 3 * hid), :], w_ff.at[num], load.at[1, num]
+        ).start()
+    out_bias, gain_two, shift_two, down_bias = (vectors[num : num + 1, :] for num in range(4))
+    og = (cot[...].astype(jnp.float32) * row_weight[...]).astype(jnp.bfloat16)
+    og_low[...] = og
+    total = None
+    for num in range(groups):
+        pltpu.make_async_copy(
+            g_in.at[num, pl.ds(out_start, hc), :], w_out.at[num], load.at[0, num]
+        ).wait()
+        part = nn_dot(att[:, num * hc : (num + 1) * hc], w_out[num])
+        total = part if total is None else total + part
+    middle = tok[...].astype(jnp.float32) + (total + out_bias)
+    centre = middle - jnp.mean(middle, -1, keepdims=True)
+    mid_scale = lax.rsqrt(jnp.mean(centre * centre, -1, keepdims=True) + norm_eps)
+    mid_hat = centre * mid_scale
+    x_two[...] = (mid_hat * gain_two + shift_two).astype(jnp.bfloat16)
+    acc[...] = middle + down_bias
+
+    def keep_mask(num):
+        lane = lax.broadcasted_iota(jnp.int32, (1, hid), 1)
+        inside = (lane < plan.hidden_cols) & (num * plan.hidden_cols + lane < FF_REAL)
+        return inside.astype(jnp.float32)
+
+    zero_col = jnp.zeros((plan.rows, 1), jnp.float32)
+
+    def expand(num, sums):
+        pltpu.make_async_copy(
+            g_in.at[num, pl.ds(ff_start, 3 * hid), :], w_ff.at[num], load.at[1, num]
+        ).wait()
+        gate = nt_dot(x_two[...], w_ff[num, 0:hid, :]) + hid_vec[num, 0:1, 0:hid]
+        up = nt_dot(x_two[...], w_ff[num, hid : 2 * hid, :]) + hid_vec[num, 1:2, 0:hid]
+        gate_s[num] = gate
+        up_s[num] = up
+        hidden = gate * jax.nn.sigmoid(gate) * up * keep_mask(num)
+        hat_s[num] = hidden
+        return (
+            sums[0] + jnp.sum(hidden, -1, keepdims=True),
+            sums[1] + jnp.sum(hidden * hidden, -1, keepdims=True),
+        )
+
+    sums = lax.fori_loop(0, groups, expand, (zero_col, zero_col))
+    mean = sums[0] / FF_REAL
+    scale = lax.rsqrt(sums[1] / FF_REAL - mean * mean + norm_eps)
+
+    def shrink(num, sums):
+        keep = keep_mask(num)
+        inner_gain = hid_vec[num, 2:3, 0:hid]
+        hat = (hat_s[num] - mean) * scale
+        low = ((hat * inner_gain + hid_vec[num, 3:4, 0:hid]) * keep).astype(jnp.bfloat16)
+        normed[num] = low
+        down = w_ff[num, 2 * hid : 3 * hid, :]
+        acc[...] += nn_dot(low, down)
+        upstream = nt_dot(og_low[...], down) * keep
+        small_h[num, 2:3, 0:hid] = jnp.sum(upstream * hat, 0, keepdims=True)
+        small_h[num, 3:4, 0:hid] = jnp.sum(upstream, 0, keepdims=True)
+        hat_grad = upstream * inner_gain
+        hat_s[num] = hat
+        grad_s[num] = hat_grad
+        return (
+            sums[0] + jnp.sum(hat_grad, -1, keepdims=True),
+            sums[1] + jnp.sum(hat_grad * hat, -1, keepdims=True),
+        )
+
+    small_h[...] = jnp.zeros_like(small_h)
+    sums = lax.fori_loop(0, groups, shrink, (zero_col, zero_col))
+    back_one, back_two = sums[0] / FF_REAL, sums[1] / FF_REAL
+    result[...] = acc[...].astype(jnp.bfloat16)
+    acc[...] = jnp.zeros_like(acc)
+
+    def spread(num, carry):
+        gate, up = gate_s[num], up_s[num]
+        hidden_grad = scale * (grad_s[num] - back_one - hat_s[num] * back_two) * keep_mask(num)
+        sig = jax.nn.sigmoid(gate)
+        gate_low = (hidden_grad * up * sig * (1.0 + gate * (1.0 - sig))).astype(jnp.bfloat16)
+        up_low = (hidden_grad * (gate * sig)).astype(jnp.bfloat16)
+        gate_g[num] = gate_low
+        up_g[num] = up_low
+        small_h[num, 0:1, 0:hid] = jnp.sum(gate_low.astype(jnp.float32), 0, keepdims=True)
+        small_h[num, 1:2, 0:hid] = jnp.sum(up_low.astype(jnp.float32), 0, keepdims=True)
+        acc[...] += nn_dot(gate_low, w_ff[num, 0:hid, :]) + nn_dot(
+            up_low, w_ff[num, hid : 2 * hid, :]
+        )
+        return carry
+
+    lax.fori_loop(0, groups, spread, 0)
+    upstream = acc[...]
+    scaled = upstream * gain_two
+    grad = og_low[...].astype(jnp.float32) + mid_scale * (
+        scaled
+        - jnp.mean(scaled, -1, keepdims=True)
+        - mid_hat * jnp.mean(scaled * mid_hat, -1, keepdims=True)
+    )
+    mid_grad[...] = grad
+    low = grad.astype(jnp.bfloat16)
+    for num, source in enumerate((x_two[...], og_low[...], low)):
+        for keeper in range(2):
+            regroup[num, keeper] = jnp.concatenate(
+                [source[:, (2 * j + keeper) * 128 : (2 * j + keeper + 1) * 128] for j in range(4)],
+                axis=1,
+            )
+    for num in range(groups):
+        att_grad[:, num * hc : (num + 1) * hc] = nt_dot(low, w_out[num]).astype(jnp.bfloat16)
+    small_a[...] = jnp.zeros_like(small_a)
+    small_a[0:1, :] = jnp.sum(low.astype(jnp.float32), 0, keepdims=True)
+    small_a[1:2, :] = jnp.sum(upstream * mid_hat, 0, keepdims=True)
+    small_a[2:3, :] = jnp.sum(upstream, 0, keepdims=True)
+    small_a[3:4, :] = jnp.sum(og_low[...].astype(jnp.float32), 0, keepdims=True)
+
+
+def block_call(plan, *operands):
+    rows, width, groups, hid = plan.rows, plan.width, plan.groups, plan.hidden
+    low, wide = jnp.bfloat16, jnp.float32
+    vmem = pl.BlockSpec(memory_space=pltpu.VMEM)
+    lanes = operands[5].shape[2]
+    return pl.pallas_call(
+        functools.partial(block_kernel, plan),
+        out_shape=(
+            jax.ShapeDtypeStruct((rows, width), low),
+            jax.ShapeDtypeStruct((rows, width), wide),
+            jax.ShapeDtypeStruct((rows, width), low),
+            jax.ShapeDtypeStruct((3, 2, rows, width // 2), low),
+            jax.ShapeDtypeStruct((groups, rows, hid), low),
+            jax.ShapeDtypeStruct((groups, rows, hid), low),
+            jax.ShapeDtypeStruct((groups, rows, hid), low),
+            jax.ShapeDtypeStruct((8, width), wide),
+            jax.ShapeDtypeStruct((groups, 8, lanes), wide),
+        ),
+        in_specs=[vmem] * 6 + [pl.BlockSpec(memory_space=pl.ANY)],
+        out_specs=(vmem,) * 9,
+        scratch_shapes=[
+            pltpu.VMEM((rows, width), low),
+            pltpu.VMEM((rows, width), low),
+            pltpu.VMEM((groups, 3 * hid, width), low),
+            pltpu.VMEM((groups, plan.head_cols, width), low),
+            pltpu.VMEM((groups, rows, hid), wide),
+            pltpu.VMEM((groups, rows, hid), wide),
+            pltpu.VMEM((groups, rows, hid), wide),
+            pltpu.VMEM((groups, rows, hid), wide),
+            pltpu.VMEM((rows, width), wide),
+            pltpu.SemaphoreType.DMA((2, groups)),
+        ],
+        compiler_params=pltpu.CompilerParams(vmem_limit_bytes=58 * 2**20),
+        name="feed_forward",
+    )(*operands)
+
+
+def backward_kernel(
+    plan,
+    att_grad,
+    qh,
+    kh,
+    vh,
+    lse,
+    kcol,
+    cos_t,
+    sin_t,
+    xg,
+    regroup,
+    normed,
+    gate_g,
+    up_g,
+    att,
+    att_own,
+    mid_grad,
+    tok,
+    gain,
+    small_a,
+    small_h,
+    g_in,
+    tok_grad,
+    grad_one,
+    grad_two,
+    grad_in,
+    sum_a,
+    sum_h,
+    sum_t,
+    w_in,
+    dog,
+    doh,
+    delta,
+    dqh,
+    dkh,
+    dvh,
+    pair,
+    dall,
+    norm_acc,
+    s_one,
+    r_one,
+    f_one,
+    e_one,
+    z_one,
+    s_two,
+    r_two,
+    f_two,
+    e_two,
+    z_two,
+    s_in,
+    r_in,
+    f_in,
+    e_in,
+    a_got,
+    h_got,
+    h_z,
+    t_got,
+    loc,
+    dog_s,
+    dog_r,
+    u_s,
+    u_r,
+    a_s,
+    a_r,
+    h_s,
+    h_r,
+    t_s,
+    t_r,
+    d_s,
+    d_r,
+):
+    rows, heads, groups = plan.rows, plan.heads, plan.groups
+    hc, hid = plan.head_cols, plan.hidden
+    pairs = heads // 2
+    dp, core, x_pos, y_pos, sib, x_nbr, y_nbr, diag = places()
+    z = lax.axis_index("tensor")
+
+    def ring(r):
+        return lax.rem(z + r, groups)
+
+    def cols(which, width):
+        return pl.ds(pl.multiple_of(which * width, 128), width)
+
+    def load_in(num):
+        return [
+            pltpu.make_async_copy(
+                g_in.at[:, pl.ds(kind * hc + num * 128, 128), :], w_in.at[:, kind], loc.at[kind]
+            )
+            for kind in range(3)
+        ]
+
+    for copy in load_in(0):
+        copy.start()
+    partners = [(sib, z), (x_nbr, z), (y_nbr, z)]
+    partners += [(dp, ring(r)) for r in range(1, groups)]
+    greet(partners)
+
+    def dog_copy(r, owner):
+        return rcopy(
+            att_grad.at[:, cols(ring(r), hc)], dog.at[owner], dog_s.at[r], dog_r.at[r], dp, ring(r)
+        )
+
+    for r in (2, 1, 3):
+        dog_copy(r, z).start()
+    dog[z] = att_grad[:, cols(z, hc)]
+
+    def a_copy(num, target):
+        return rcopy(sum_a, a_got.at[num], a_s.at[num], a_r.at[num], target, z)
+
+    def h_copy(num, target):
+        return rcopy(h_got.at[3], h_got.at[num], h_s.at[num], h_r.at[num], target, z)
+
+    sum_a[...] = small_a[...]
+    h_got[3] = small_h[...]
+    plane = (sib, x_nbr, y_nbr)
+    a_copy(0, sib).start()
+    h_copy(0, sib).start()
+
+    def small_step(num):
+        a_copy(num, plane[num]).wait()
+        h_copy(num, plane[num]).wait()
+        sum_a[...] += a_got[num]
+        h_got[3] += h_got[num]
+        if num < 2:
+            a_copy(num + 1, plane[num + 1]).start()
+            h_copy(num + 1, plane[num + 1]).start()
+
+    order = (2, 1, 3, 0)
+
+    class Unit:
+        def __init__(self, num, x_first, send, held, first, second):
+            self.num, self.x_first = num, x_first
+            self.send, self.held, self.first, self.second = send, held, first, second
+            self.a, self.b = (x_pos, y_pos) if x_first else (y_pos, x_pos)
+            self.near, self.far = (x_nbr, y_nbr) if x_first else (y_nbr, x_nbr)
+
+        def copies(self, hop):
+            src, dst, target = (
+                (self.send, self.held, sib),
+                (self.held.at[1 - self.a], self.first, self.near),
+                (self.held.at[self.a, 1 - self.b], self.second, self.far),
+            )[hop]
+            return rcopy(src, dst, u_s.at[self.num, hop], u_r.at[self.num, hop], target, z)
+
+        def put(self, into, start, value, add):
+            for j in range(4):
+                y_of, x_of = divmod(j, 2)
+                spot = (x_of, y_of) if self.x_first else (y_of, x_of)
+                place = pl.ds(start, value.shape[0])
+                cut = value[:, j * 128 : (j + 1) * 128]
+                if add:
+                    cut = cut + self.held[spot[0], spot[1], place, :].astype(jnp.float32)
+                into[spot[0], spot[1], place, :] = cut.astype(jnp.bfloat16)
+
+        def second_hop(self):
+            self.copies(1).wait_recv()
+            self.held[self.a, 1 - self.b] += self.first[1 - self.b]
+            self.copies(2).start()
+            self.held[self.a, self.b] += self.first[self.b]
+
+        def total(self):
+            self.copies(2).wait_recv()
+            return self.held[self.a, self.b].astype(jnp.float32) + self.second[...].astype(
+                jnp.float32
+            )
+
+        def sent(self):
+            for hop in range(3):
+                if hop > 0 or self.num >= 4:
+                    self.copies(hop).wait_send()
+
+    units = []
+    for step in range(groups):
+        even = step % 2 == 0
+        slot = step % 2
+        units.append(
+            (
+                Unit(
+                    2 * step, even, s_one.at[slot], r_one.at[step], f_one.at[step], e_one.at[step]
+                ),
+                Unit(
+                    2 * step + 1,
+                    not even,
+                    s_two.at[slot],
+                    r_two.at[step],
+                    f_two.at[step],
+                    e_two.at[step],
+                ),
+            )
+        )
+
+    def fill(step, keeper, add):
+        target = ring(order[step])
+        one, two = units[step]
+        into_one = one.held if add else one.send
+        into_two = two.held if add else two.send
+        x_part, og_part, mid_part = (regroup[num, keeper] for num in range(3))
+        one.put(into_one, 0, tn_dot(gate_g[target], x_part), add)
+        one.put(into_one, hid, tn_dot(att[:, cols(target, hc)], mid_part), add)
+        if add:
+            one.copies(1).start()
+        else:
+            one.copies(0).start()
+        two.put(into_two, 0, tn_dot(up_g[target], x_part), add)
+        two.put(into_two, hid, tn_dot(normed[target], og_part), add)
+        if add:
+            two.copies(1).start()
+        else:
+            two.copies(0).start()
+
+    def give(step):
+        if step >= 2:
+            for unit in units[step - 2]:
+                unit.copies(0).wait_send()
+        fill(step, 1 - core, False)
+
+    def keep(step):
+        for unit in units[step]:
+            unit.copies(0).wait_recv()
+        fill(step, core, True)
+
+    def second(step):
+        for unit in units[step]:
+            unit.second_hop()
+
+    def z_copies(step, owner):
+        r = order[step]
+        pieces = []
+        for num, (unit, got) in enumerate(zip(units[step], (z_one, z_two))):
+            pieces.append(
+                rcopy(
+                    unit.held.at[unit.a, unit.b],
+                    got.at[r],
+                    d_s.at[num, r],
+                    d_r.at[num, r],
+                    dp,
+                    owner,
+                )
+            )
+        return pieces
+
+    def along_z(step):
+        for unit in units[step]:
+            unit.held[unit.a, unit.b] = unit.total().astype(jnp.bfloat16)
+        for copy in z_copies(step, ring(order[step])):
+            copy.start()
+
+    give(0)
+    give(1)
+    small_step(0)
+    keep(0)
+    give(2)
+    keep(1)
+    give(3)
+    small_step(1)
+    keep(2)
+    keep(3)
+
+    for r in range(1, groups):
+        dog_copy(r, lax.rem(z + groups - r, groups)).wait()
+    selector = (
+        lax.broadcasted_iota(jnp.int32, (8, hc), 1) // DH
+        == lax.broadcasted_iota(jnp.int32, (8, hc), 0)
+    ).astype(jnp.float32)
+    all_dog = dog[...].reshape(groups * rows, hc)
+    all_own = att_own[...].reshape(groups * rows, hc)
+    delta[...] = lax.dot_general(
+        selector,
+        all_dog.astype(jnp.float32) * all_own.astype(jnp.float32),
+        (((1,), (1,)), ((), ())),
+        precision=lax.Precision.HIGHEST,
+        preferred_element_type=jnp.float32,
+    )
+    for head in range(heads):
+        doh[head] = all_dog[:, head * DH : (head + 1) * DH]
+    small_step(2)
+
+    def z_small(r):
+        return (
+            rcopy(sum_a, a_got.at[3 + z], a_s.at[2 + r], a_r.at[2 + r], dp, ring(r)),
+            rcopy(h_got.at[3, ring(r)], h_z.at[z], h_s.at[2 + r], h_r.at[2 + r], dp, ring(r)),
+        )
+
+    for r in range(1, groups):
+        for copy in z_small(r):
+            copy.start()
+    a_got[3 + z] = sum_a[...]
+    h_z[z] = h_got[3, z]
+
+    def head_step(head, block):
+        place = pl.ds(pl.multiple_of(block * rows, 16), rows)
+        spot = lax.rem(head, 2)
+        queries = qh[head]
+        upstream = doh[head]
+        keys = kh[head, place, :]
+        row_dots = delta[pl.ds(head, 1), :]
+        scores = nt_dot(keys, queries) * (0.125 * LOG2E) + kcol[place, :] - lse[head]
+        probs = jnp.exp2(scores)
+        dvh[spot, place, :] = nn_dot(probs.astype(jnp.bfloat16), upstream)
+        prob_grad = nt_dot(vh[head, place, :], upstream)
+        score_grad = (probs * (prob_grad - row_dots)).astype(jnp.bfloat16)
+        dkh[spot, place, :] = nn_dot(score_grad, queries) * 0.125
+        part = tn_dot(score_grad, keys) * 0.125
+
+        @pl.when(block == 0)
+        def _():
+            dqh[spot] = part
+
+        @pl.when(block > 0)
+        def _():
+            dqh[spot] += part
+
+    in_units = []
+    for num in range(pairs):
+        for half in range(2):
+            place = 2 * num + half
+            in_units.append(
+                Unit(
+                    2 * groups + place,
+                    half == 0,
+                    s_in.at[place],
+                    r_in.at[place],
+                    f_in.at[place],
+                    e_in.at[place],
+                )
+            )
+
+    def pair_copies(num, r, owner):
+        target = ring(r)
+        lanes = pl.ds(num * 128, 128)
+        return rcopy(
+            pair.at[num, :, pl.ds(pl.multiple_of(target * rows, 16), rows), :],
+            dall.at[owner, :, :, lanes],
+            d_s.at[2 + num, r],
+            d_r.at[2 + num, r],
+            dp,
+            target,
+        )
+
+    def finish_pair(num):
+        def joined(source):
+            return jnp.concatenate([source[0], source[1]], axis=1)
+
+        def turned_back(values):
+            return values * cos_t[...] - lane_swap(values) * sin_t[...]
+
+        query_low = turned_back(joined(dqh)).astype(jnp.bfloat16)
+        key_low = turned_back(joined(dkh)).astype(jnp.bfloat16)
+        value_low = joined(dvh).astype(jnp.bfloat16)
+        for kind, low in enumerate((query_low, key_low, value_low)):
+            pair[num, kind] = low
+        for r in (2, 1, 3):
+            pair_copies(num, r, z).start()
+        for kind in range(3):
+            dall[z, kind, :, num * 128 : (num + 1) * 128] = pair[
+                num, kind, pl.ds(pl.multiple_of(z * rows, 16), rows), :
+            ]
+        own = cols(2 * z + num, 128)
+        sum_t[2:3, own] = jnp.sum(query_low.astype(jnp.float32), 0, keepdims=True)
+        sum_t[3:4, own] = jnp.sum(value_low.astype(jnp.float32), 0, keepdims=True)
+
+    def in_fill(num, keeper, add):
+        values = jnp.concatenate(
+            [
+                jnp.concatenate([xg[num, :, cols(2 * j + keeper, 128)] for j in range(4)], axis=1)
+                for num in range(groups)
+            ],
+            axis=0,
+        )
+        for kind in range(3):
+            value = tn_dot(pair[num, kind], values)
+            for half in range(2):
+                unit = in_units[2 * num + half]
+                into = unit.held if add else unit.send
+                unit.put(into, kind * DH, value[half * DH : (half + 1) * DH], add)
+        for half in range(2):
+            in_units[2 * num + half].copies(1 if add else 0).start()
+
+    def in_give(num):
+        in_fill(num, 1 - core, False)
+
+    def in_keep(num):
+        for half in range(2):
+            in_units[2 * num + half].copies(0).wait_recv()
+        in_fill(num, core, True)
+
+    def in_second(num):
+        for half in range(2):
+            in_units[2 * num + half].second_hop()
+
+    def in_total(num):
+        for half in range(2):
+            grad_in[2 * num + half] = in_units[2 * num + half].total()
+
+    def norm_part(num):
+        for r in range(1, groups):
+            pair_copies(num, r, lax.rem(z + groups - r, groups)).wait_recv()
+        for copy in load_in(num):
+            copy.wait()
+        total = None
+        for num_z in range(groups):
+            for kind in range(3):
+                part = nn_dot(
+                    dall[num_z, kind, :, num * 128 : (num + 1) * 128],
+                    w_in[num_z, kind],
+                )
+                total = part if total is None else total + part
+        return total
+
+    sum_t[...] = jnp.zeros_like(sum_t)
+    plans = {
+        1: lambda: second(0),
+        4: lambda: along_z(0),
+        7: lambda: (finish_pair(0), in_give(0)),
+        8: lambda: second(1),
+        9: lambda: in_keep(0),
+        11: lambda: along_z(1),
+        13: lambda: in_second(0),
+        15: lambda: (finish_pair(1), in_give(1)),
+    }
+
+    @pl.loop(0, heads * groups)
+    def _(turn):
+        head_step(turn // groups, lax.rem(turn, groups))
+        for at, work in plans.items():
+            pl.when(turn == at)(lambda work=work: (work(), None)[1])
+
+    norm_acc[...] = norm_part(0)
+    for copy in load_in(1):
+        copy.start()
+    second(2)
+    in_keep(1)
+    in_total(0)
+    along_z(2)
+    upstream = norm_acc[...] + norm_part(1)
+    wide = tok[...].astype(jnp.float32)
+    centre = wide - jnp.mean(wide, -1, keepdims=True)
+    scale = lax.rsqrt(jnp.mean(centre * centre, -1, keepdims=True) + norm_eps)
+    hat = centre * scale
+    scaled = upstream * gain[...]
+    tok_grad[...] = mid_grad[...] + scale * (
+        scaled
+        - jnp.mean(scaled, -1, keepdims=True)
+        - hat * jnp.mean(scaled * hat, -1, keepdims=True)
+    )
+    sum_t[0:1, :] = jnp.sum(upstream * hat, 0, keepdims=True)
+    sum_t[1:2, :] = jnp.sum(upstream, 0, keepdims=True)
+
+    def t_copy(num, target, target_z):
+        return rcopy(sum_t, t_got.at[num], t_s.at[num], t_r.at[num], target, target_z)
+
+    def t_step(num):
+        t_copy(num, plane[num], z).wait()
+        sum_t[...] += t_got[num]
+        if num < 2:
+            t_copy(num + 1, plane[num + 1], z).start()
+
+    def t_along(r):
+        return rcopy(sum_t, t_got.at[3 + z], t_s.at[2 + r], t_r.at[2 + r], dp, ring(r))
+
+    t_copy(0, sib, z).start()
+    in_second(1)
+    t_step(0)
+    second(3)
+    t_step(1)
+    in_total(1)
+    t_step(2)
+    for r in range(1, groups):
+        t_along(r).start()
+    t_got[3 + z] = sum_t[...]
+
+    for r in range(1, groups):
+        for copy in z_small(r):
+            copy.wait()
+    sum_a[...] = (a_got[3] + a_got[4]) + (a_got[5] + a_got[6])
+    sum_h[...] = (h_z[0] + h_z[1]) + (h_z[2] + h_z[3])
+
+    one, two = units[groups - 1]
+    for num, (unit, got, out) in enumerate(((one, z_one, grad_one), (two, z_two, grad_two))):
+        total = unit.total()
+        for step in range(groups - 1):
+            z_copies(step, ring(order[step]))[num].wait_recv()
+            total = total + got[order[step]].astype(jnp.float32)
+        out[...] = total
+
+    for r in range(1, groups):
+        t_along(r).wait()
+    sum_t[...] = (t_got[3] + t_got[4]) + (t_got[5] + t_got[6])
+    for both in units:
+        for unit in both:
+            unit.sent()
+    for unit in in_units:
+        unit.sent()
+    for step in range(groups - 1):
+        for copy in z_copies(step, ring(order[step])):
+            copy.wait_send()
+    for num in range(pairs):
+        for r in range(1, groups):
+            pair_copies(num, r, z).wait_send()
+
+
+def backward_call(plan, *operands):
+    rows, seq, heads, groups = plan.rows, plan.seq, plan.heads, plan.groups
+    hc, hid, width = plan.head_cols, plan.hidden, plan.width
+    pairs = heads // 2
+    low, wide = jnp.bfloat16, jnp.float32
+    lanes = operands[19].shape[2]
+    one, two = hid + hc, 2 * hid
+    vmem = pl.BlockSpec(memory_space=pltpu.VMEM)
+    dma = pltpu.SemaphoreType.DMA
+    in_rows = 3 * DH
+    return pl.pallas_call(
+        functools.partial(backward_kernel, plan),
+        out_shape=(
+            jax.ShapeDtypeStruct((rows, width), wide),
+            jax.ShapeDtypeStruct((one, 128), wide),
+            jax.ShapeDtypeStruct((two, 128), wide),
+            jax.ShapeDtypeStruct((heads, in_rows, 128), wide),
+            jax.ShapeDtypeStruct((8, width), wide),
+            jax.ShapeDtypeStruct((8, lanes), wide),
+            jax.ShapeDtypeStruct((8, width), wide),
+        ),
+        in_specs=[vmem] * 20 + [pl.BlockSpec(memory_space=pl.ANY)],
+        out_specs=(vmem,) * 7,
+        scratch_shapes=[
+            pltpu.VMEM((groups, 3, 128, width), low),
+            pltpu.VMEM((groups, rows, hc), low),
+            pltpu.VMEM((heads, seq, DH), low),
+            pltpu.VMEM((8, seq), wide),
+            pltpu.VMEM((2, seq, DH), wide),
+            pltpu.VMEM((2, seq, DH), wide),
+            pltpu.VMEM((2, seq, DH), wide),
+            pltpu.VMEM((pairs, 3, seq, 128), low),
+            pltpu.VMEM((groups, 3, rows, hc), low),
+            pltpu.VMEM((rows, width), wide),
+            pltpu.VMEM((2, 2, 2, one, 128), low),
+            pltpu.VMEM((groups, 2, 2, one, 128), low),
+            pltpu.VMEM((groups, 2, one, 128), low),
+            pltpu.VMEM((groups, one, 128), low),
+            pltpu.VMEM((groups, one, 128), low),
+            pltpu.VMEM((2, 2, 2, two, 128), low),
+            pltpu.VMEM((groups, 2, 2, two, 128), low),
+            pltpu.VMEM((groups, 2, two, 128), low),
+            pltpu.VMEM((groups, two, 128), low),
+            pltpu.VMEM((groups, two, 128), low),
+            pltpu.VMEM((heads, 2, 2, in_rows, 128), low),
+            pltpu.VMEM((heads, 2, 2, in_rows, 128), low),
+            pltpu.VMEM((heads, 2, in_rows, 128), low),
+            pltpu.VMEM((heads, in_rows, 128), low),
+            pltpu.VMEM((3 + groups, 8, width), wide),
+            pltpu.VMEM((4, groups, 8, lanes), wide),
+            pltpu.VMEM((groups, 8, lanes), wide),
+            pltpu.VMEM((3 + groups, 8, width), wide),
+            dma((3,)),
+            dma((groups,)),
+            dma((groups,)),
+            dma((2 * groups + heads, 3)),
+            dma((2 * groups + heads, 3)),
+            dma((2 + groups,)),
+            dma((2 + groups,)),
+            dma((2 + groups,)),
+            dma((2 + groups,)),
+            dma((2 + groups,)),
+            dma((2 + groups,)),
+            dma((2 + pairs, groups)),
+            dma((2 + pairs, groups)),
+        ],
+        compiler_params=pltpu.CompilerParams(
+            collective_id=1, has_side_effects=True, vmem_limit_bytes=62 * 2**20
+        ),
+        name="attend_back_reduce",
+    )(*operands)
+
+
+def fast_device(
+    tokens,
+    cotangent,
+    image_valid,
+    key_mask,
+    patch_rows,
+    patch_cols,
+    first_gain,
+    first_bias,
+    input_weight,
+    input_bias,
+    output_weight,
+    output_bias,
+    second_gain,
+    second_bias,
+    expand_weight,
+    expand_bias,
+    inner_gain,
+    inner_bias,
+    shrink_weight,
+    shrink_bias,
+):
+    local_rows, images, width = tokens.shape
+    head_cols, hidden_cols = input_weight.shape[2], expand_weight.shape[2]
+    plan = Plan(local_rows, width, head_cols, hidden_cols, lax.axis_size("tensor"))
+    rank = lax.axis_index("tensor")
+    tok = pad_rows(tokens.reshape(local_rows, width), plan.rows)
+    cot = pad_rows(cotangent.reshape(local_rows, width), plan.rows)
+    packed = pack_weights(input_weight, output_weight, expand_weight, shrink_weight, plan)
+    hid_vec = hidden_vectors(expand_bias, inner_gain, inner_bias, plan)
+    cos_t, sin_t = rotation_tables(patch_rows, patch_cols, plan, 2 * DH)
+    kbias = jnp.where(by_group(key_mask, plan).reshape(1, -1) > 0, 0.0, masked_score)
+    position = rank * local_rows + jnp.arange(plan.rows)
+    row_weight = (position < LEN).astype(jnp.float32) * image_valid.astype(jnp.float32)
+    vectors = jnp.stack([output_bias, second_gain, second_bias, shrink_bias])
+    weights, att, rows_one, qh, kh, vh, lse, hid_all, att_own = forward_call(
+        plan,
+        tok,
+        first_gain[None],
+        first_bias[None],
+        packed,
+        hid_vec,
+        cos_t,
+        sin_t,
+        kbias,
+        input_bias,
+    )
+    (
+        result,
+        mid_grad,
+        att_grad,
+        regroup,
+        normed,
+        gate_g,
+        up_g,
+        small_a,
+        small_h,
+    ) = block_call(plan, tok, att, cot, row_weight[:, None], vectors, hid_all, weights)
+    tok_grad, grad_one, grad_two, grad_in, sum_a, sum_h, sum_t = backward_call(
+        plan,
+        att_grad,
+        qh,
+        kh,
+        vh,
+        lse.reshape(plan.heads, 1, plan.seq),
+        kbias.reshape(plan.seq, 1),
+        cos_t,
+        sin_t,
+        rows_one,
+        regroup,
+        normed,
+        gate_g,
+        up_g,
+        att,
+        att_own,
+        mid_grad,
+        tok,
+        first_gain[None],
+        small_a,
+        small_h,
+        weights,
+    )
+    in_grad = grad_in.reshape(plan.heads, 3, DH, -1).transpose(1, 3, 0, 2)
+    expand_grad = jnp.stack([grad_one[:hidden_cols].T, grad_two[:hidden_cols].T])
+    return (
+        result[:local_rows].reshape(local_rows, images, width),
+        tok_grad[:local_rows].reshape(local_rows, images, width),
+        sum_t[0],
+        sum_t[1],
+        in_grad.reshape(3, -1, head_cols),
+        lax.dynamic_slice_in_dim(sum_t[2:4], rank * head_cols, head_cols, 1),
+        grad_one[plan.hidden :],
+        sum_a[0],
+        sum_a[1],
+        sum_a[2],
+        expand_grad,
+        sum_h[0:2, :hidden_cols],
+        sum_h[2, :hidden_cols],
+        sum_h[3, :hidden_cols],
+        grad_two[plan.hidden : plan.hidden + hidden_cols],
+        sum_a[3],
+    )
+
+
 def solution(mesh):
+    kernels_fit = mesh.shape["dp"] == 8 and mesh.shape["tensor"] == 4
     return jax.shard_map(
-        on_device,
+        fast_device if kernels_fit else on_device,
         mesh=mesh,
         in_specs=(
             P("tensor", "dp", None),

time: 1370 us -> 400 us (0.29)
  waiting for transfers between devices: 921 us -> 0 us
  Pallas kernels: 0 us -> 365 us
  blocking collectives: 125 us -> 0 us
  matrix products: 98.4 us -> 0 us
  other arithmetic: 94.2 us -> 7.03 us
  local copies, waits for them, and re-layouts: 94.9 us -> 18.8 us
  between operations: 17.9 us -> 2.07 us
    pallas_call x0 -> x3, Pallas kernels: none -> 365 us  [the longest x1 184 us: backward_call(): pl.pallas_call(functools.partial(backward_kernel, plan), out_shape=(jax.S...]
    all_gather x7 -> x0, waiting for transfers between devices: 336 us -> none  [the longest x1 81.5 us: on_device(): lax.all_gather(out_grad_low, 'tensor', axis=0, tiled=True)]
    unnamed x18 -> x0, waiting for transfers between devices: 313 us -> none
    reduce_scatter x4 -> x0, waiting for transfers between devices: 195 us -> none  [the longest x1 57.8 us: on_device(): lax.psum_scatter(expand_grad, 'dp', scatter_dimension=1, tiled=True)]
    dot_general x33 -> x0, matrix products: 98.4 us -> none  [the longest x2 11.4 us: on_device(): jnp.einsum('pihc,kihc->ihpk', grad_block, values, preferred_element_type=...]
    psum x1 -> x0, waiting for transfers between devices: 77.6 us -> none  [on_device(): lax.psum((shared_parts, placed_heads, placed_hidden), ('dp', 'tensor'))]
    unnamed x1 -> x0, blocking collectives: 77.3 us -> none
    reduce_sum x12 -> x0, other arithmetic: 49.4 us -> none  [the longest x2 8.42 us: row_norm(): scale = lax.rsqrt(jnp.mean(centre * centre, -1, keepdims=True) + norm_eps)]
  transfers between devices with their start and end apart: 16 -> 0, of which waited for: 15 -> 0; matrix products, arithmetic and copies ran while one was open for 6% -> 0% of each run, Pallas kernels for 0% -> 0%
where the time goes in v1:
time: 400 us; the launch traced here: 393 us
  Pallas kernels  365 us (91%)
  local copies, waits for them, and re-layouts  18.8 us (5%)
  other arithmetic  7.03 us (2%)
    pallas_call x1, Pallas kernels, backward_call(): pl.pallas_call(functools.partial(backward_kernel, plan), out_shape=(jax.S...  184 us
    pallas_call x1, Pallas kernels, forward_call(): pl.pallas_call(functools.partial(forward_kernel, plan), out_shape=(jax.Sh...  157 us
    pallas_call x1, Pallas kernels, block_call(): pl.pallas_call(functools.partial(block_kernel, plan), out_shape=(jax.Shap...  24.5 us

profile of v1, /device:TPU:0, one launch (start us, length us, event | category | flops | bytes accessed | tf_op | source)
XLA Modules:
  0.0 392.9 jit_solution(7703400309984288131)
XLA Ops:
  0.6 0.0 copy-start.6
  0.7 0.0 copy-start.7
  0.7 0.0 copy-start.5
  0.7 2.0 pad.29.tok
  2.6 0.0 copy-start.13
  2.7 1.1 copy.49
  3.8 0.0 copy-done.5
  3.8 0.0 copy-start.14
  3.8 0.2 copy.41
  4.0 0.0 copy-done.6
  4.0 0.0 copy-done.7
  4.0 0.9 fusion.3.wpk
  4.9 0.0 copy-done.15
  4.9 0.0 copy-done.16
  4.9 0.0 copy-done.10
  5.0 0.6 select_maximum_fusion.sml
  5.6 0.0 copy-done.12
  5.6 0.1 reshape.183
  5.7 0.1 broadcast_in_dim.63
  5.8 0.0 copy-done.13
  5.8 0.1 reshape.182
  5.9 0.1 broadcast_in_dim.61
  6.0 0.0 copy-start.2
  6.0 3.3 sine_multiply_fusion
  9.4 0.0 copy-done.14
  9.4 0.1 reshape.184
  9.5 0.7 select_n.75.kbias
  10.2 156.8 %gather_attend.1 = (bf16[4,3088,1024]{2,1,0:T(8,128)(2,1)}, bf16[272,1024]{1,0:T(8,128)(2,1)}, bf16[4,272,1024]{2,1,0:T(8,128)(2,1)}, bf16[4,1088,64]{2,1,0:T(8,...) custom-call(bf16[272,1024]{1,0:T(8,128)(2,1)} %pad.29.tok, ...), custom_call_target="tpu_custom_call" | custom-call | tf_op jit(solution)/shard_map/gather_attend/pallas_call | solution.py:783
  167.0 0.0 copy-done.2
  167.0 0.8 pad.36.cot
  168.5 0.7 fusion.5.row_weight
  169.2 0.0 copy-done.17
  169.2 0.0 copy-done.18
  169.2 0.0 copy-done.19
  169.2 0.0 copy-done.20
  169.2 0.6 pad_maximum_fusion.1.vectors
  169.9 24.5 %feed_forward.1 = (bf16[272,1024]{1,0:T(8,128)(2,1)}, f32[272,1024]{1,0:T(8,128)}, bf16[272,1024]{1,0:T(8,128)(2,1)}, bf16[3,2,272,512]{3,2,1,0:T(8,128)(2,1)}, ...) custom-call(bf16[272,1024]{1,0:T(8,128)(2,1)} %pad.29.tok, ...), custom_call_target="tpu_custom_call" | custom-call | tf_op jit(solution)/shard_map/feed_forward/pallas_call | solution.py:1009
  194.4 1.9 slice_bitcast_fusion.1
  196.3 0.0 copy-done
  196.3 0.7 reduce.3
  197.0 0.6 reshape.191.lse
  197.6 1.0 select_n.78.kcol
  198.6 183.6 %attend_back_reduce.1 = (f32[272,1024]{1,0:T(8,128)}, f32[944,128]{1,0:T(8,128)}, f32[1376,128]{1,0:T(8,128)}, f32[4,192,128]{2,1,0:T(8,128)}, f32[8,1024]{1,0:T...) custom-call(bf16[272,1024]{1,0:T(8,128)(2,1)} %get-tuple-element.45.att_grad, bf16[4,1088,64]{2,1,0:T(8,128)(2,1)} %get-tuple-element.46.qh, ...), custom_call_target="tpu_custom_call" | custom-call | tf_op jit(solution)/shard_map/attend_back_reduce/pallas_call | solution.py:1553
  382.3 1.3 slice_bitcast_fusion
  383.6 0.0 copy-start.9
  383.6 0.0 copy-start.4
  383.6 0.0 copy-start.3
  383.6 0.0 copy-start.8
  383.6 0.0 copy-start.1
  383.7 2.1 copy.46
  385.7 0.0 copy-done.9
  385.7 0.6 fusion.13
  386.3 0.0 copy-done.4
  386.4 0.9 copy.47
  387.3 0.6 constant_dynamic-slice_fusion
  387.9 0.0 copy-done.3
  387.9 0.7 slice.53
  388.5 0.0 copy-done.8
  388.5 0.6 fusion.12
  389.1 0.0 copy-done.1
  389.1 0.8 fusion.11
  390.0 1.2 copy.48
  391.2 0.6 slice.59
  391.8 0.6 slice_reduce_fusion
  (26 shorter events, 0.3 us)
Async XLA Ops:
  0.6 3.3 copy-start.6
  0.7 3.3 copy-start.7
  0.7 3.1 copy-start.5
  2.6 2.3 copy-start.15
  2.6 2.3 copy-start.16
  2.6 2.3 copy-start.10
  2.6 3.0 copy-start.12
  2.6 3.2 copy-start.13
  3.8 5.6 %copy-start.14 = (s32[1,1028]{1,0:T(1,128)S(1)}, s32[1,1028]{1,0:T(1,128)}, u32[]{:S(2)}) copy-start(s32[1,1028]{1,0:T(1,128)} %param.23) | copy-start | bytes 12340
  6.0 161.0 %copy-start.2 = (bf16[257,1,1024]{2,0,1:T(8,128)(2,1)S(1)}, bf16[257,1,1024]{2,0,1:T(8,128)(2,1)}, u32[]{:S(2)}) copy-start(bf16[257,1,1024]{2,0,1:T(8,128)(2,1)} %param.21) | copy-start | bytes 1579012
  10.2 159.1 %copy-start.17 = (f32[1024]{0:T(1024)S(1)}, f32[1024]{0:T(1024)}, u32[]{:S(2)}) copy-start(f32[1024]{0:T(1024)} %param.39) | copy-start | bytes 12292
  10.2 159.1 %copy-start.18 = (f32[1024]{0:T(1024)S(1)}, f32[1024]{0:T(1024)}, u32[]{:S(2)}) copy-start(f32[1024]{0:T(1024)} %param.33) | copy-start | bytes 12292
  10.2 159.1 %copy-start.19 = (f32[1024]{0:T(1024)S(1)}, f32[1024]{0:T(1024)}, u32[]{:S(2)}) copy-start(f32[1024]{0:T(1024)} %param.32) | copy-start | bytes 12292
  10.2 159.1 %copy-start.20 = (f32[1024]{0:T(1024)S(1)}, f32[1024]{0:T(1024)}, u32[]{:S(2)}) copy-start(f32[1024]{0:T(1024)} %param.31) | copy-start | bytes 12292
  169.9 26.4 %copy-start = (f32[4,1088,1]{2,1,0:T(8,128)S(1)}, f32[4,1088,1]{2,1,0:T(8,128)}, u32[]{:S(2)}) copy-start(f32[4,1088,1]{2,1,0:T(8,128)} %get-tuple-element.49) | copy-start | bytes 52228
  383.6 2.1 copy-start.9
  383.6 2.7 copy-start.4
  383.6 4.2 %copy-start.3 = (f32[944,128]{1,0:T(8,128)S(1)}, f32[944,128]{1,0:T(8,128)}, u32[]{:S(2)}) copy-start(f32[944,128]{1,0:T(8,128)} %get-tuple-element.62) | copy-start | bytes 1449988
  383.6 4.9 %copy-start.8 = (f32[8,1024]{1,0:T(8,128)S(1)}, f32[8,1024]{1,0:T(8,128)}, u32[]{:S(2)}) copy-start(f32[8,1024]{1,0:T(8,128)} %get-tuple-element.63) | copy-start | bytes 98308
  383.6 5.5 %copy-start.1 = (f32[1376,128]{1,0:T(8,128)S(1)}, f32[1376,128]{1,0:T(8,128)}, u32[]{:S(2)}) copy-start(f32[1376,128]{1,0:T(8,128)} %get-tuple-element.64) | copy-start | bytes 2113540
  389.9 1.3 copy-start.11
